TPU v7x, 32 devices: a whole 2x2x4 slice. The times are simulated.
32 devices in a mesh: ctx: 16 (over z, y, core), mp: 2 (over x).
Axes of the slice: x: 2, y: 2, z: 4, core: 2. Of those that a mesh axis runs over, the one named last changes fastest.
Arguments:
- sublayer_input: bfloat16 [2048, 4096], P('ctx'), may hold values from -6 to 6
- rotated_queries: bfloat16 [2048, 8192], P('ctx', 'mp'), may hold values from -5 to 5
- rotated_keys: bfloat16 [2048, 1024], P('ctx', 'mp'), may hold values from -5 to 5
- output_grad: bfloat16 [2048, 8192], P('ctx', 'mp'), may hold values from -6 to 6
- value_weight: bfloat16 [4096, 1024], P(None, 'mp'), may hold values from -0.09375 to 0.09375
- segment_ids: int32 [2048], replicated, may hold values from 0 to 3, never falling along the last dimension, each value on 1 to 1536 neighbouring positions
- label_positions: int32 [128], replicated, may hold values from 0 to 2047
Outputs:
- query_grad: bfloat16 [2048, 8192], P('ctx', 'mp')
- key_grad: bfloat16 [2048, 1024], P('ctx', 'mp')
- input_grad: bfloat16 [2048, 4096], P('ctx', 'mp')
- value_weight_grad: bfloat16 [4096, 1024], P('ctx', 'mp')
Inputs may be any that keep to these rules, and one draw needn't show every extreme that they name: `segment_ids`: ids never fall along the slab; one trace takes exactly 1536 positions. `label_positions`: a position may appear more than once.
All inputs are finite; a program needn't handle non-finite values.
Results may differ from a plain program's by a relative error of at most 0.017.
Values may be sent and summed in bfloat16 or wider, within the bound.
A program may use at most 64 MiB of HBM per device.

v0:
```python
import jax
import jax.numpy as jnp
from jax import lax
from jax.sharding import PartitionSpec as P

HEADS = 64
KV_HEADS = 8
HD = 128


NEGATIVE = -1e30


def from_partner(value, axis, distance):
    mask = 2**distance
    pairs = [(source, source ^ mask) for source in range(lax.axis_size(axis))]
    return lax.ppermute(value, axis, pairs)


def halve_sum(blocks_view, context_index):
    bit_count = blocks_view.shape[0].bit_length() - 1
    target_index = context_index ^ 1
    current = blocks_view
    for bit_index in reversed(range(bit_count)):
        half_count = current.shape[0] // 2
        lower_half = current[:half_count]
        upper_half = current[half_count:]
        upper_mine = target_index >> bit_index & 1 == 1
        keep_part = jnp.where(upper_mine, upper_half, lower_half)
        send_part = jnp.where(upper_mine, lower_half, upper_half)
        current = keep_part + from_partner(send_part, "ctx", bit_index)
    return from_partner(current[0].astype(jnp.bfloat16), "ctx", 0).astype(jnp.float32)


def on_device(
    sublayer_input,
    rotated_queries,
    rotated_keys,
    output_grad,
    value_weight,
    segment_ids,
    label_positions,
):
    local_rows = sublayer_input.shape[0]
    context_count = lax.axis_size("ctx")
    context_index = lax.axis_index("ctx")
    total_rows = local_rows * context_count
    group_size = HEADS // KV_HEADS
    local_heads = rotated_keys.shape[1] // HD
    score_scale = HD ** (-0.5)
    key_width = 512
    first_row = context_index * local_rows
    own_positions = first_row + jnp.arange(local_rows, dtype=jnp.int32)
    labelled = jnp.any(own_positions[:, None] == label_positions[None, :], axis=1)
    loss_weight = jnp.where(labelled, 4.0, 1.0).astype(jnp.float32)
    weighted = (output_grad.astype(jnp.float32) * loss_weight[:, None]).astype(jnp.bfloat16)
    values = jnp.dot(sublayer_input, value_weight, preferred_element_type=jnp.float32).astype(
        jnp.bfloat16
    )
    all_keys, all_values = (
        lax.all_gather(rotated_keys, "ctx", axis=0, tiled=True),
        lax.all_gather(values, "ctx", axis=0, tiled=True),
    )
    query_four = rotated_queries.reshape(local_rows, local_heads, group_size, HD)
    grad_four = weighted.reshape(local_rows, local_heads, group_size, HD)
    own_segments = lax.dynamic_slice_in_dim(segment_ids, first_row, local_rows)
    every_position = jnp.arange(total_rows, dtype=jnp.int32)
    doc_begin = jnp.min(jnp.where(segment_ids == own_segments[0], every_position, total_rows))
    lower_block = doc_begin // key_width
    upper_block = (first_row + local_rows - 1) // key_width + 1

    def block_terms(block_index):
        block_start = block_index * key_width
        key_part = lax.dynamic_slice_in_dim(all_keys, block_start, key_width, 0).reshape(
            key_width, local_heads, HD
        )
        value_part = lax.dynamic_slice_in_dim(all_values, block_start, key_width, 0).reshape(
            key_width, local_heads, HD
        )
        key_positions = block_start + jnp.arange(key_width, dtype=jnp.int32)
        key_segments = lax.dynamic_slice_in_dim(segment_ids, block_start, key_width)
        allowed = (own_segments[:, None] == key_segments[None, :]) & (
            own_positions[:, None] >= key_positions[None, :]
        )
        allowed = allowed[None, None, :, :]
        scores = (
            jnp.einsum("tcgd,kcd->cgtk", query_four, key_part, preferred_element_type=jnp.float32)
            * score_scale
        )
        grad_probs = jnp.einsum(
            "tcgd,kcd->cgtk", grad_four, value_part, preferred_element_type=jnp.float32
        )
        masked = jnp.where(allowed, scores, NEGATIVE)
        return (block_start, key_part, allowed, masked, grad_probs)

    def first_pass(block_index, carry):
        running_max, running_sum, running_dot = carry
        block_start, key_part, allowed, masked, grad_probs = block_terms(block_index)
        new_max = jnp.maximum(running_max, jnp.max(masked, axis=-1))
        factor = jnp.exp(running_max - new_max)
        weights = jnp.where(allowed, jnp.exp(masked - new_max[..., None]), 0.0)
        new_sum = running_sum * factor + jnp.sum(weights, axis=-1)
        new_dot = running_dot * factor + jnp.sum(weights * grad_probs, axis=-1)
        return (new_max, new_sum, new_dot)

    stat_shape = (local_heads, group_size, local_rows)
    start_stats = (
        jnp.full(stat_shape, NEGATIVE, jnp.float32),
        jnp.zeros(stat_shape, jnp.float32),
        jnp.zeros(stat_shape, jnp.float32),
    )
    running_max, running_sum, running_dot = lax.fori_loop(
        lower_block, upper_block, first_pass, start_stats
    )
    log_total = running_max + jnp.log(running_sum)
    delta = running_dot / running_sum

    def second_pass(block_index, carry):
        query_sum, grad_buffer = carry
        block_start, key_part, allowed, masked, grad_probs = block_terms(block_index)
        probabilities = jnp.where(allowed, jnp.exp(masked - log_total[..., None]), 0.0)
        probs_low = probabilities.astype(jnp.bfloat16)
        grad_scores = (probabilities * (grad_probs - delta[..., None]) * score_scale).astype(
            jnp.bfloat16
        )
        query_sum = query_sum + jnp.einsum(
            "cgtk,kcd->tcgd", grad_scores, key_part, preferred_element_type=jnp.float32
        )
        key_term = jnp.einsum(
            "cgtk,tcgd->kcd", grad_scores, query_four, preferred_element_type=jnp.float32
        )
        value_term = jnp.einsum(
            "cgtk,tcgd->kcd", probs_low, grad_four, preferred_element_type=jnp.float32
        )
        joined = jnp.concatenate(
            [
                key_term.reshape(key_width, local_heads * HD),
                value_term.reshape(key_width, local_heads * HD),
            ],
            axis=1,
        )
        grad_buffer = lax.dynamic_update_slice_in_dim(grad_buffer, joined, block_start, 0)
        return (query_sum, grad_buffer)

    start_query = jnp.zeros((local_rows, local_heads, group_size, HD), jnp.float32)
    start_buffer = jnp.zeros((total_rows, 2 * local_heads * HD), jnp.float32)
    query_sum, grad_buffer = lax.fori_loop(
        lower_block, upper_block, second_pass, (start_query, start_buffer)
    )
    query_grad = query_sum.reshape(local_rows, local_heads * group_size * HD).astype(jnp.bfloat16)
    blocks_view = grad_buffer.reshape(context_count, local_rows, 2 * local_heads * HD)
    summed = halve_sum(blocks_view, context_index)
    key_grad = summed[:, : local_heads * HD].astype(jnp.bfloat16)
    value_grad = summed[:, local_heads * HD :].astype(jnp.bfloat16)
    input_term = lax.dot_general(
        value_grad, value_weight, (((1,), (1,)), ((), ())), preferred_element_type=jnp.float32
    )
    input_grad = lax.psum_scatter(
        input_term.astype(jnp.bfloat16), "mp", scatter_dimension=1, tiled=True
    )
    value_weight_grad = lax.psum_scatter(
        lax.dot_general(
            sublayer_input, value_grad, (((0,), (0,)), ((), ())), preferred_element_type=jnp.float32
        ),
        "ctx",
        scatter_dimension=0,
        tiled=True,
    ).astype(jnp.bfloat16)
    return (query_grad, key_grad, input_grad, value_weight_grad)


def solution(mesh):
    placed = (
        P("ctx", None),
        P("ctx", "mp"),
        P("ctx", "mp"),
        P("ctx", "mp"),
        P(None, "mp"),
        P(),
        P(),
    )
    return jax.shard_map(
        on_device,
        mesh=mesh,
        in_specs=placed,
        out_specs=(P("ctx", "mp"), P("ctx", "mp"), P("ctx", "mp"), P("ctx", "mp")),
        check_vma=False,
    )
```

profile of v0, /device:TPU:0, one launch (start us, length us, event | category | flops | bytes accessed | tf_op | source)
XLA Modules:
  0.0 572.7 jit_solution(4602272268060936328)
XLA Ops:
  8.4 3.6 convolution_convert_fusion.1
  18.8 1.6 copy.55
  21.1 35.2 %all-gather.5.cloned.1.call-done = bf16[2048,512]{1,0:T(8,128)(2,1)} async-done(((bf16[128,512]{1,0:T(8,128)(2,1)}), bf16[2048,512]{1,0:T(8,128)(2,1)}) %all-gather.5.cloned.1.call-update) | async-done | bytes 2097168 | tf_op jit(solution)/shard_map/all_gather | solution.py:62
  56.2 3.9 copy.58
  60.2 38.8 %all-gather.3.cloned.1.call-done = bf16[2048,512]{0,1:T(8,128)(2,1)} async-done(((bf16[128,512]{0,1:T(8,128)(2,1)}), bf16[2048,512]{0,1:T(8,128)(2,1)}) %all-gather.3.cloned.1.call-update) | async-done | bytes 2097168 | tf_op jit(solution)/shard_map/all_gather | solution.py:61
  99.0 8.2 %while.28 = (s32[]{:T(128)}, f32[4,8,128]{2,1,0:T(8,128)S(1)}, f32[4,8,128]{2,1,0:T(8,128)S(1)}, f32[4,8,128]{2,1,0:T(8,128)S(1)}, s32[]{:T(128)}, /*index=5*/s3...) while((s32[]{:T(128)}, f32[4,8,128]{2,1,0:T(8,128)S(1)}, ...), condition=%wide.region_6.7_spmd.clone, body=%wide.region_2.6_spmd.clone.sunk | while | flops 1103311488 | bytes 35172080 | solution.py:112
  102.1 3.0 fusion.69
  105.1 2.1 fusion.70
  107.2 1.6 broadcast_in_dim.70
  108.8 4.3 broadcast_in_dim.71
  113.1 13.5 %while.29 = (s32[]{:T(128)}, f32[128,4,8,128]{0,3,2,1:T(8,128)}, f32[2048,1024]{0,1:T(8,128)}, s32[]{:T(128)}, bf16[2048,512]{0,1:T(8,128)(2,1)}, /*index=5*/s32...) while((s32[]{:T(128)}, f32[128,4,8,128]{0,3,2,1:T(8,128)}, ...), condition=%wide.region_8.9_spmd.clone, body=%wide.region_7.8_spmd.clone.sunk | while | flops 2712863232 | bytes 73133840 | solution.py:147
  116.0 2.3 fusion.83
  118.3 3.4 fusion.82
  124.5 1.7 maximum_dynamic-update-slice_fusion.2
  126.6 8.6 %slice_select_fusion = (f32[1024,1024]{0,1:T(8,128)}, f32[1024,1024]{0,1:T(8,128)}) fusion(f32[2048,1024]{0,1:T(8,128)} %get-tuple-element.142, pred[]{:T(512)S(6)} %eq.73), kind=kLoop, calls=%fused_computation.39 | loop fusion | flops 2097152 | bytes 16777216 | tf_op jit(solution)/shard_map/jit(_where)/select_n | solution.py:30
  135.2 5.4 copy.63
  140.6 44.7 %collective-permute-start = (f32[8,128,1024]{2,1,0:T(8,128)}, f32[8,128,1024]{2,1,0:T(8,128)}, u32[]{:S(2)}, u32[]{:S(2)}) collective-permute-start(f32[8,128,1024]{2,1,0:T(8,128)} %bitcast.165), channel_id=1, source_target_pairs={{0,16},{2,18},{4,20},{6,22},{8,24},{10,26},{12,28},{14,30},{16,0},... | collective-permute-start | bytes 12582920 | tf_op jit(solution)/shard_map/ppermute | solution.py:17
  185.3 5.4 copy.62
  190.7 155.6 %collective-permute-done = f32[8,128,1024]{2,1,0:T(8,128)} collective-permute-done((f32[8,128,1024]{2,1,0:T(8,128)}, f32[8,128,1024]{2,1,0:T(8,128)}, u32[]{:S(2)}, u32[]{:S(2)}) %collective-permute-start) | collective-permute-done | bytes 4194336 | tf_op jit(solution)/shard_map/ppermute | solution.py:17
  346.3 4.4 add.92
  350.7 2.0 copy-done.4
  353.2 47.7 %collective-permute-done.1 = f32[4,128,1024]{2,1,0:T(8,128)} collective-permute-done((f32[4,128,1024]{2,1,0:T(8,128)S(1)}, f32[4,128,1024]{2,1,0:T(8,128)}, u32[]{:S(2)}, u32[]{:S(2)}) %collective-permute-start.1) | collective-permute-done | bytes 2097184 | tf_op jit(solution)/shard_map/ppermute | solution.py:17
  400.9 3.5 select_add_fusion
  405.5 1.7 collective-permute-start.2
  407.3 22.9 %collective-permute-done.2 = f32[2,128,1024]{2,1,0:T(8,128)} collective-permute-done((f32[2,128,1024]{2,1,0:T(8,128)}, f32[2,128,1024]{2,1,0:T(8,128)}, u32[]{:S(2)}, u32[]{:S(2)}) %collective-permute-start.2) | collective-permute-done | bytes 1048608 | tf_op jit(solution)/shard_map/ppermute | solution.py:17
  430.1 1.5 select_add_fusion.1
  431.8 1.9 collective-permute-done.3
  435.4 4.5 convolution_bitcast_fusion
  440.0 4.9 convolution_convert_fusion
  446.1 2.4 copy.77
  449.1 94.3 %reduce-scatter.5.cloned.1.call-done = f32[256,512]{0,1:T(8,128)} async-done(((f32[4096,512]{0,1:T(8,128)}), f32[256,512]{0,1:T(8,128)}) %reduce-scatter.5.cloned.1.call-update) | async-done | bytes 524304 | tf_op jit(solution)/shard_map/reduce_scatter | solution.py:161
  545.3 20.9 %reduce-scatter.3.cloned.1.call-done = bf16[128,2048]{1,0:T(8,128)(2,1)} async-done(((bf16[128,4096]{1,0:T(8,128)(2,1)}), bf16[128,2048]{1,0:T(8,128)(2,1)}) %reduce-scatter.3.cloned.1.call-update) | async-done | bytes 524304 | tf_op jit(solution)/shard_map/reduce_scatter | solution.py:158
  (74 shorter events, 22.3 us)
Async XLA Ops:
  7.2 1.2 copy-start
  7.2 4.9 copy-start.9
  7.2 5.7 copy-start.10
  7.2 9.1 %copy-start.11 = (s32[128]{0:T(128)S(1)}, s32[128]{0:T(128)}, u32[]{:S(2)}) copy-start(s32[128]{0:T(128)} %param.17) | copy-start | bytes 1540
  7.2 9.3 %copy-start.7 = (bf16[128,4096]{1,0:T(8,128)(2,1)S(1)}, bf16[128,4096]{1,0:T(8,128)(2,1)}, u32[]{:S(2)}) copy-start(bf16[128,4096]{1,0:T(8,128)(2,1)} %param.14) | copy-start | bytes 3145732
  7.2 49.0 %all-gather.5.cloned.1.call-start = ((), (), s32[]{:S(2)}) async-start(), calls=%async_computation.3 | async-start | bytes 2228224 | tf_op jit(solution)/shard_map/all_gather | solution.py:62
  12.0 87.0 %all-gather.3.cloned.1.call-start = ((), (), s32[]{:S(2)}) async-start(), calls=%async_computation.2 | async-start | bytes 2228224 | tf_op jit(solution)/shard_map/all_gather | solution.py:61
  12.8 530.6 %reduce-scatter.5.cloned.1.call-start = ((), (), s32[]{:S(2)}) async-start(), calls=%async_computation.5 | async-start | bytes 8912896 | tf_op jit(solution)/shard_map/reduce_scatter | solution.py:161
  17.4 3.0 copy-start.5
  100.6 1.5 copy-start.8
  108.8 4.3 copy-start.6
  121.7 1.6 copy-start.1
  124.5 2.1 copy-start.2
  140.6 205.7 %collective-permute-start = (f32[8,128,1024]{2,1,0:T(8,128)}, f32[8,128,1024]{2,1,0:T(8,128)}, u32[]{:S(2)}, u32[]{:S(2)}) collective-permute-start(f32[8,128,1024]{2,1,0:T(8,128)} %bitcast.165), channel_id=1, source_target_pairs={{0,16},{2,18},{4,20},{6,22},{8,24},{10,26},{12,28},{14,30},{16,0},... | collective-permute-start | bytes 12582920 | tf_op jit(solution)/shard_map/ppermute | solution.py:17
  350.7 2.0 copy-start.4
  353.1 47.8 %collective-permute-start.1 = (f32[4,128,1024]{2,1,0:T(8,128)S(1)}, f32[4,128,1024]{2,1,0:T(8,128)}, u32[]{:S(2)}, u32[]{:S(2)}) collective-permute-start(f32[4,128,1024]{2,1,0:T(8,128)S(1)} %slice_select_fusion.2), channel_id=1, source_target_pairs={{0,8},{2,10},{4,12},{6,14},{8,0},{10,2},{12,4},{14,6},{16,24},{18,... | collective-permute-start | bytes 6291464 | tf_op jit(solution)/shard_map/ppermute | solution.py:17
  405.5 24.6 %collective-permute-start.2 = (f32[2,128,1024]{2,1,0:T(8,128)}, f32[2,128,1024]{2,1,0:T(8,128)}, u32[]{:S(2)}, u32[]{:S(2)}) collective-permute-start(f32[2,128,1024]{2,1,0:T(8,128)} %slice_select_fusion.3), channel_id=1, source_target_pairs={{0,4},{2,6},{4,0},{6,2},{8,12},{10,14},{12,8},{14,10},{16,20},{18,... | collective-permute-start | bytes 3145736 | tf_op jit(solution)/shard_map/ppermute | solution.py:17
  431.7 2.0 collective-permute-start.3
  433.8 1.6 collective-permute-start.4
  440.0 5.0 copy-start.3
  440.0 126.2 %reduce-scatter.3.cloned.1.call-start = ((), (), s32[]{:S(2)}) async-start(), calls=%async_computation.4 | async-start | bytes 1572864 | tf_op jit(solution)/shard_map/reduce_scatter | solution.py:158
Sparse Core Ops, SparseCore 0:
  12.1 44.0 all-gather.4
  59.0 39.9 all-gather.2
  440.1 103.2 reduce-scatter.4
  546.1 20.0 reduce-scatter.2
where the time goes:
time: 573 us
  waiting for transfers between devices  419 us (73%)
  starting transfers between devices  47 us (8%)
  local copies, waits for them, and re-layouts  35.9 us (6%)
  other arithmetic  27.3 us (5%)
  matrix products  27.1 us (5%)
  between operations  16.6 us (3%)
    ppermute x5, waiting for transfers between devices, from_partner(): return lax.ppermute(value, axis, pairs)  229 us
    reduce_scatter x1, waiting for transfers between devices, on_device(): lax.psum_scatter(lax.dot_general(sublayer_input, value_grad, (((0,), (0,)...  94.3 us
    ppermute x5, starting transfers between devices, from_partner(): return lax.ppermute(value, axis, pairs)  46.8 us
    all_gather x1, waiting for transfers between devices, on_device(): lax.all_gather(rotated_keys, 'ctx', axis=0, tiled=True)  38.8 us
    all_gather x1, waiting for transfers between devices, on_device(): lax.all_gather(values, 'ctx', axis=0, tiled=True)  35.2 us
    reduce_scatter x1, waiting for transfers between devices, on_device(): lax.psum_scatter(input_term.astype(jnp.bfloat16), 'mp', scatter_dimension...  20.9 us
    unnamed x24, local copies, waits for them, and re-layouts  12.3 us
  transfers between devices with their start and end apart: 9, of which 9 were waited for; matrix products, arithmetic and copies ran while one was open for 5% of the time, Pallas kernels for 0%

commit v1 on v0

v1 whole, which is shorter than its diff:
```python
import functools

import jax
import jax.numpy as jnp
from jax import lax
from jax.experimental import pallas as pl
from jax.experimental.pallas import tpu as pltpu
from jax.sharding import PartitionSpec as P

HEADS = 64
KV_HEADS = 8
HD = 128
GROUP = HEADS // KV_HEADS
SCALE = HD ** (-0.5)
LOG2E = 1.4426950408889634
NEGATIVE = -1e30
MESH = pl.DeviceIdType.MESH
SLAB = 4
CORE = 1
SIDE = 2
BF = jnp.bfloat16
F32 = jnp.float32
VMEM_LIMIT = 56 * 1024 * 1024


def remote(src, dst, send, recv, axis, index):
    return pltpu.make_async_remote_copy(
        src_ref=src,
        dst_ref=dst,
        send_sem=send,
        recv_sem=recv,
        device_id={axis: index},
        device_id_type=MESH,
    )


def flip(pos, bit):
    if bit == CORE:
        return pos + 1 - 2 * lax.rem(pos, 2)
    return lax.rem(pos + 2, SLAB)


def dot(a, b):
    return jnp.dot(a, b, preferred_element_type=F32)


def greet(me, count, mp_count):
    barrier = pltpu.get_barrier_semaphore()

    def along(d, _):
        peer = lax.rem(me + d, count)
        pl.semaphore_signal(barrier, inc=1, device_id={"ctx": peer}, device_id_type=MESH)
        return 0

    lax.fori_loop(1, count, along, 0)
    mine = lax.axis_index("mp")
    for d in range(1, mp_count):
        peer = lax.rem(mine + d, mp_count)
        pl.semaphore_signal(barrier, inc=1, device_id={"mp": peer}, device_id_type=MESH)
    pl.semaphore_wait(barrier, count - 1 + mp_count - 1)


def repeat(low, high, body):
    def step(i, _):
        body(i)
        return 0

    lax.fori_loop(low, high, step, 0)


def kernel(
    count, mp_count, heads, keep, x_split,
    begin_ref, weight_ref, q_ref, g_ref, k_ref, v_ref, x_ref, w_ref,
    dq_ref, dk_ref, ig_ref, wg_ref,
    kv, part, rc, ry, rz, sy, sz, all_v, pair, xc, xt, wr,
    qs, qt, gs, gt, top, total, dotted, dq_acc, pb, sb, block_top, e_all, p_all, ig_acc,
    g_recv, g_send, rc_sem, ry_sem, rz_sem, sc_sem, sy_sem, sz_sem,
    ag_recv, ag_send, mp_recv, mp_send, x_recv, x_send, xf_recv, xf_send,
    w_recv, w_send, w_own,
):
    rows = q_ref.shape[0]
    wide = 2 * rows
    kb = 2 * rows
    slabs = count // SLAB
    me = lax.axis_index("ctx")
    mine = lax.axis_index("mp")
    slab = me // SLAB
    pos = lax.rem(me, SLAB)
    base = me - pos
    core_pos, side_pos = flip(pos, CORE), flip(pos, SIDE)
    both_pos = flip(side_pos, CORE)
    last = slab == slabs - 1
    first_row = me * rows
    blocks = me // 2 + 1
    greet(me, count, mp_count)

    w_rows = w_ref.shape[0] // mp_count

    def weight_copy(peer, slot):
        at = pl.ds(pl.multiple_of(peer * w_rows, w_rows), w_rows)
        return remote(w_ref.at[at, :], wr.at[slot], w_send.at[peer], w_recv.at[slot], "mp", peer)

    def gather_copy(c, dest, block):
        target = (me + SLAB, base + side_pos, base + core_pos)[dest]
        ref = kv.at[c, block]
        return remote(ref, ref, g_send.at[c, dest, block], g_recv.at[c, block], "ctx", target)

    def gather_own(c):
        cols = pl.ds(pl.multiple_of(c * HD, HD), HD)
        kv[c, me, :, :HD] = k_ref[:, cols]
        kv[c, me, :, HD:] = v_ref[:, cols]

        @pl.when(slab < slabs - 1)
        def _():
            gather_copy(c, 0, me).start()

        gather_copy(c, 1, me).start()
        gather_copy(c, 2, me).start()

    def gather_forward(c):
        def one(k):
            block = (slab - k) * SLAB + pos
            gather_copy(c, 0, block).wait_recv()

            @pl.when(slab < slabs - 1)
            def _():
                gather_copy(c, 0, block).start()

            gather_copy(c, 1, block).start()
            gather_copy(c, 2, block).start()

        repeat(1, slab + 1, one)

    def gather_cross(c):
        def one(k):
            block = (slab - k) * SLAB + side_pos
            gather_copy(c, 1, block).wait_recv()
            gather_copy(c, 2, block).start()

        repeat(0, slab + 1, one)

    def gather_arrive(c):
        def one(s):
            gather_copy(c, 2, s * SLAB + core_pos).wait_recv()
            gather_copy(c, 2, s * SLAB + both_pos).wait_recv()

        repeat(0, slab + 1, one)

    def gather_finish(c):
        def one(s):
            @pl.when(slab < slabs - 1)
            def _():
                gather_copy(c, 0, s * SLAB + pos).wait_send()

            gather_copy(c, 1, s * SLAB + pos).wait_send()
            gather_copy(c, 2, s * SLAB + pos).wait_send()
            gather_copy(c, 2, s * SLAB + side_pos).wait_send()

        repeat(0, slab + 1, one)

    def core_copy(c, which, s):
        block = s * SLAB + (core_pos, both_pos)[which]
        return remote(
            part.at[c, block], rc.at[c, which, s],
            sc_sem.at[c, which, s], rc_sem.at[c, which, s], "ctx", base + core_pos,
        )

    def side_copy(c, s):
        return remote(
            sy.at[c, s], ry.at[c, s], sy_sem.at[c, s], ry_sem.at[c, s], "ctx", base + side_pos
        )

    def down_copy(c, s):
        return remote(
            sz.at[c, s], rz.at[c, s], sz_sem.at[c, s], rz_sem.at[c, s], "ctx", me - SLAB
        )

    def reduce_core(c):
        def one(s):
            core_copy(c, 1, s).start()
            core_copy(c, 0, s).start()

        repeat(0, slab + 1, one)

    def reduce_side(c):
        def one(s):
            core_copy(c, 1, s).wait_recv()
            both = part[c, s * SLAB + side_pos].astype(F32) + rc[c, 1, s].astype(F32)
            sy[c, s] = both.astype(BF)
            side_copy(c, s).start()

        repeat(0, slab + 1, one)

    def slab_total(c, s):
        core_copy(c, 0, s).wait_recv()
        both = part[c, s * SLAB + pos].astype(F32) + rc[c, 0, s].astype(F32)
        side_copy(c, s).wait_recv()
        return both + ry[c, s].astype(F32)

    def reduce_down(c):
        def deliver(s, full):
            @pl.when(s < slab)
            def _():
                sz[c, s] = full.astype(BF)
                down_copy(c, s).start()

            @pl.when(s == slab)
            def _():
                low = full.astype(BF)
                dk_ref[:, pl.ds(pl.multiple_of(c * HD, HD), HD)] = low[:, :HD]
                all_v[c, me] = low[:, HD:]
                pair[mine, c] = low[:, HD:]

        def one(s):
            full = slab_total(c, s)

            @pl.when(slab < slabs - 1)
            def _():
                down_copy(c, s).wait_recv()
                deliver(s, full + rz[c, s].astype(F32))

            @pl.when(last)
            def _():
                deliver(s, full)

        repeat(0, slab + 1, one)
        for d in range(1, mp_count):
            peer = lax.rem(mine + d, mp_count)
            pair_copy(c, peer, mine).start()

        @pl.when(slab < slabs - 1)
        def _():
            spread_copy(c, 0, me).start()

        @pl.when(slab > 0)
        def _():
            spread_copy(c, 1, me).start()

        spread_copy(c, 2, me).start()
        spread_copy(c, 3, me).start()

    def reduce_finish(c):
        def one(s):
            core_copy(c, 0, s).wait_send()
            core_copy(c, 1, s).wait_send()
            side_copy(c, s).wait_send()

            @pl.when(s < slab)
            def _():
                down_copy(c, s).wait_send()

        repeat(0, slab + 1, one)

    def pair_copy(c, peer, slot):
        return remote(
            all_v.at[c, me], pair.at[slot, c], mp_send.at[c, peer], mp_recv.at[c, slot],
            "mp", peer,
        )

    def spread_copy(c, dest, block):
        target = (me + SLAB, me - SLAB, base + side_pos, base + core_pos)[dest]
        ref = all_v.at[c, block]
        return remote(ref, ref, ag_send.at[c, dest, block], ag_recv.at[c, block], "ctx", target)

    def spread_forward(c):
        def one(k):
            low, high = slab - k, slab + k

            @pl.when(high < slabs)
            def _():
                block = high * SLAB + pos
                spread_copy(c, 0, block).wait_recv()

                @pl.when(slab > 0)
                def _():
                    spread_copy(c, 1, block).start()

                spread_copy(c, 2, block).start()
                spread_copy(c, 3, block).start()

            @pl.when(low >= 0)
            def _():
                block = low * SLAB + pos
                spread_copy(c, 0, block).wait_recv()

                @pl.when(slab < slabs - 1)
                def _():
                    spread_copy(c, 0, block).start()

                spread_copy(c, 2, block).start()
                spread_copy(c, 3, block).start()

        repeat(1, slabs, one)

    def spread_cross(c):
        def one(s):
            block = s * SLAB + side_pos
            spread_copy(c, 2, block).wait_recv()
            spread_copy(c, 3, block).start()

        repeat(0, slabs, one)

    def spread_arrive(c):
        def one(s):
            spread_copy(c, 3, s * SLAB + core_pos).wait_recv()
            spread_copy(c, 3, s * SLAB + both_pos).wait_recv()

        repeat(0, slabs, one)

    def spread_finish(c):
        def one(s):
            own = s * SLAB + pos

            @pl.when((s <= slab) & (slab < slabs - 1))
            def _():
                spread_copy(c, 0, own).wait_send()

            @pl.when((s >= slab) & (slab > 0))
            def _():
                spread_copy(c, 1, own).wait_send()

            spread_copy(c, 2, own).wait_send()
            spread_copy(c, 3, own).wait_send()
            spread_copy(c, 3, s * SLAB + side_pos).wait_send()

        repeat(0, slabs, one)

    owner = lax.rem(me, mp_count) == mine
    x_cols = xc.shape[2]

    def x_piece(t):
        if x_split:
            return x_ref.at[t]
        return x_ref.at[:, pl.ds(pl.multiple_of(t * x_cols, x_cols), x_cols)]

    def x_copy(t, slot):
        return remote(x_piece(t), xc.at[slot], x_send.at[t], x_recv.at[slot], "ctx", t)

    def x_start():
        @pl.when(owner)
        def _():
            xc[me] = x_piece(me)[...]

        def one(i):
            t = lax.rem(i * mp_count + mine + (me // mp_count) * mp_count, count)

            @pl.when(t != me)
            def _():
                x_copy(t, me).start()

        repeat(0, count // mp_count, one)

    def x_over(peer):
        return remote(xc, xc, xf_send.at[peer], xf_recv, "mp", peer)

    def x_forward():
        @pl.when(owner)
        def _():
            def one(d):
                peer = lax.rem(me + d, count)
                x_copy(peer, peer).wait_recv()

            repeat(1, count, one)
            for d in range(1, mp_count):
                x_over(lax.rem(mine + d, mp_count)).start()

    def x_arrive():
        if mp_count > 1:
            @pl.when(jnp.logical_not(owner))
            def _():
                x_over(lax.rem(mine + 1, mp_count)).wait_recv()

    def x_finish():
        def one(i):
            t = i * mp_count + mine

            @pl.when(t != me)
            def _():
                x_copy(t, me).wait_send()

        repeat(0, count // mp_count, one)

        @pl.when(owner)
        def _():
            for d in range(1, mp_count):
                x_over(lax.rem(mine + d, mp_count)).wait_send()

    begin = begin_ref[...]
    row_at = first_row + lax.broadcasted_iota(jnp.int32, (1, rows), 1)

    def visible(j):
        at = j * kb + lax.broadcasted_iota(jnp.int32, (kb, rows), 0)
        seen = (at >= begin) & (at <= row_at)
        return jnp.concatenate([seen, seen], axis=1)

    def key_block(c, j):
        return kv[c, pl.ds(2 * j, 2), :, :HD].reshape(kb, HD)

    def value_block(c, j):
        return kv[c, pl.ds(2 * j, 2), :, HD:].reshape(kb, HD)

    def terms(c, j, seen, span):
        scores = dot(key_block(c, j), qt[:, span]) * (SCALE * LOG2E)
        return jnp.where(seen, scores, NEGATIVE), dot(value_block(c, j), gt[:, span])

    def prepare(c):
        for g in range(GROUP):
            cols = pl.ds(pl.multiple_of((c * GROUP + g) * HD, HD), HD)
            span = slice(g * rows, (g + 1) * rows)
            q = q_ref[:, cols]
            grad = (g_ref[:, cols].astype(F32) * weight_ref[...]).astype(BF)
            qs[span, :] = q
            gs[span, :] = grad
            qt[:, span] = q.T
            gt[:, span] = grad.T
        dq_acc[...] = jnp.zeros_like(dq_acc)
        top[...] = jnp.full_like(top, NEGATIVE)
        total[...] = jnp.zeros_like(total)
        dotted[...] = jnp.zeros_like(dotted)

    def first_pass(c):
        def one(j):
            seen = visible(j)
            for tile in range(GROUP // 2):
                span = slice(tile * wide, (tile + 1) * wide)
                scores, grad_probs = terms(c, j, seen, span)
                old = top[:, span]
                new = jnp.maximum(old, jnp.max(scores, axis=0, keepdims=True))
                e = jnp.exp2(scores - new)
                factor = jnp.exp2(old - new)
                top[:, span] = new
                total[:, span] = total[:, span] * factor + jnp.sum(e, axis=0, keepdims=True)
                dotted[:, span] = dotted[:, span] * factor + jnp.sum(
                    e * grad_probs, axis=0, keepdims=True
                )
                if keep:
                    block_top[j, :, span] = new
                    e_all[j, :, span] = e
                    p_all[j, :, span] = grad_probs

        repeat(0, blocks, one)
        total[...] = 1.0 / total[...]
        dotted[...] = dotted[...] * total[...]

    def second_pass(c):
        for i in range(SLAB):
            part[c, base + i] = jnp.zeros((rows, 2 * HD), BF)

        def one(j):
            if not keep:
                seen = visible(j)
            for tile in range(GROUP // 2):
                span = slice(tile * wide, (tile + 1) * wide)
                if keep:
                    ratio = jnp.exp2(block_top[j, :, span] - top[:, span]) * total[:, span]
                    probs = e_all[j, :, span] * ratio
                    grad_probs = p_all[j, :, span]
                else:
                    scores, grad_probs = terms(c, j, seen, span)
                    probs = jnp.exp2(scores - top[:, span]) * total[:, span]
                pb[:, span] = probs.astype(BF)
                sb[:, span] = (probs * (grad_probs - dotted[:, span])).astype(BF)
            low = sb[...]
            at = pl.ds(2 * j, 2)
            value_term = dot(pb[...], gs[...]).astype(BF)
            key_term = (dot(low, qs[...]) * SCALE).astype(BF)
            part[c, at, :, HD:] = value_term.reshape(2, rows, HD)
            part[c, at, :, :HD] = key_term.reshape(2, rows, HD)
            dq_acc[...] += dot(key_block(c, j).T, low)

        repeat(0, blocks, one)
        for g in range(GROUP):
            cols = pl.ds(pl.multiple_of((c * GROUP + g) * HD, HD), HD)
            dq_ref[:, cols] = (dq_acc[:, g * rows:(g + 1) * rows] * SCALE).T.astype(BF)

    repeat(0, heads, gather_own)
    for d in range(1, mp_count):
        weight_copy(lax.rem(mine + d, mp_count), mine).start()
    own_rows = pl.ds(pl.multiple_of(mine * w_rows, w_rows), w_rows)
    own_weight = pltpu.make_async_copy(w_ref.at[own_rows, :], wr.at[mine], w_own)
    own_weight.start()
    early = slab < slabs // 2
    ahead = jnp.where(early, heads, 1)

    def gather_both(c):
        gather_forward(c)
        gather_cross(c)

    repeat(0, ahead, gather_both)

    def head(c):
        prepare(c)
        gather_arrive(c)

        @pl.when(c == min(1, heads - 1))
        def _():
            x_start()

        first_pass(c)

        @pl.when((c < heads - 1) & jnp.logical_not(early))
        def _():
            gather_forward(c + 1)

        @pl.when(c > 0)
        def _():
            reduce_side(c - 1)

        second_pass(c)
        reduce_core(c)

        @pl.when((c < heads - 1) & jnp.logical_not(early))
        def _():
            gather_cross(c + 1)

        @pl.when(c > 0)
        def _():
            reduce_down(c - 1)

        @pl.when(c > 1)
        def _():
            spread_forward(c - 2)

    repeat(0, heads, head)
    final = heads - 1
    reduce_side(final)
    x_forward()
    reduce_down(final)
    if heads > 1:
        spread_forward(heads - 2)
    spread_forward(final)

    repeat(0, heads, spread_cross)
    x_arrive()
    for i in range(count):
        xt[:, i * rows:(i + 1) * rows] = xc[i].T
    own_weight.wait()
    for d in range(1, mp_count):
        peer = lax.rem(mine + d, mp_count)
        weight_copy(peer, peer).wait_recv()
        for c in range(heads):
            pair_copy(c, peer, peer).wait_recv()

    contract = (((1,), (1,)), ((), ()))

    def input_term(m):
        for c in range(heads):
            term = lax.dot_general(
                pair[m, c], wr[m, :, c * HD:(c + 1) * HD], contract,
                preferred_element_type=F32,
            )
            ig_acc[...] += term

    ig_acc[...] = jnp.zeros_like(ig_acc)
    repeat(0, mp_count, input_term)
    ig_ref[...] = ig_acc[...].astype(BF)
    for c in range(heads):
        spread_arrive(c)
        wg_ref[:, c * HD:(c + 1) * HD] = dot(
            xt[...], all_v[c].reshape(count * rows, HD)
        ).astype(BF)

    for d in range(1, mp_count):
        peer = lax.rem(mine + d, mp_count)
        weight_copy(peer, mine).wait_send()
        for c in range(heads):
            pair_copy(c, peer, mine).wait_send()
    x_finish()
    repeat(0, heads, gather_finish)
    repeat(0, heads, reduce_finish)
    repeat(0, heads, spread_finish)


def on_device(
    sublayer_input, rotated_queries, rotated_keys, output_grad, value_weight,
    segment_ids, label_positions,
):
    rows, features = sublayer_input.shape
    count = lax.axis_size("ctx")
    mp_count = lax.axis_size("mp")
    slabs = count // SLAB
    total_rows = rows * count
    width = rotated_keys.shape[1]
    heads = width // HD
    span = GROUP * rows
    kb = 2 * rows
    first_row = lax.axis_index("ctx") * rows
    own = first_row + jnp.arange(rows, dtype=jnp.int32)
    labelled = jnp.any(own[:, None] == label_positions[None, :], axis=1)
    weight = jnp.where(labelled, 4.0, 1.0).astype(F32)[:, None]
    own_segments = lax.dynamic_slice_in_dim(segment_ids, first_row, rows)
    begin = jnp.sum(
        (segment_ids[:, None] < own_segments[None, :]).astype(jnp.int32), axis=0, dtype=jnp.int32
    )
    values = dot(sublayer_input, value_weight).astype(BF)
    x_cols = features // count
    x_split = x_cols % 128 != 0
    pieces = sublayer_input
    if x_split:
        pieces = sublayer_input.reshape(rows, count, x_cols).transpose(1, 0, 2)
    keep = total_rows <= 4096
    kept = (total_rows // kb, kb, span) if keep else (1, 8, 128)
    vmem = pl.BlockSpec(memory_space=pltpu.VMEM)
    anywhere = pl.BlockSpec(memory_space=pl.ANY)
    dma = pltpu.SemaphoreType.DMA
    chunk = (rows, 2 * HD)
    pairs = rows * GROUP * heads * total_rows
    return pl.pallas_call(
        functools.partial(kernel, count, mp_count, heads, keep, x_split),
        out_shape=(
            jax.ShapeDtypeStruct(rotated_queries.shape, BF),
            jax.ShapeDtypeStruct((rows, width), BF),
            jax.ShapeDtypeStruct((rows, features // mp_count), BF),
            jax.ShapeDtypeStruct((x_cols, width), BF),
        ),
        in_specs=[vmem] * 7 + [anywhere],
        out_specs=(vmem,) * 4,
        scratch_shapes=[
            pltpu.VMEM((heads, count) + chunk, BF),
            pltpu.VMEM((heads, count) + chunk, BF),
            pltpu.VMEM((heads, 2, slabs) + chunk, BF),
            pltpu.VMEM((heads, slabs) + chunk, BF),
            pltpu.VMEM((heads, slabs) + chunk, BF),
            pltpu.VMEM((heads, slabs) + chunk, BF),
            pltpu.VMEM((heads, slabs) + chunk, BF),
            pltpu.VMEM((heads, count, rows, HD), BF),
            pltpu.VMEM((mp_count, heads, rows, HD), BF),
            pltpu.VMEM((count, rows, x_cols), BF),
            pltpu.VMEM((x_cols, total_rows), BF),
            pltpu.VMEM((mp_count, features // mp_count, width), BF),
            pltpu.VMEM((span, HD), BF),
            pltpu.VMEM((HD, span), BF),
            pltpu.VMEM((span, HD), BF),
            pltpu.VMEM((HD, span), BF),
            pltpu.VMEM((1, span), F32),
            pltpu.VMEM((1, span), F32),
            pltpu.VMEM((1, span), F32),
            pltpu.VMEM((HD, span), F32),
            pltpu.VMEM((kb, span), BF),
            pltpu.VMEM((kb, span), BF),
            pltpu.VMEM((total_rows // kb, 1, span), F32),
            pltpu.VMEM(kept, F32),
            pltpu.VMEM(kept, F32),
            pltpu.VMEM((rows, features // mp_count), F32),
            dma((heads, count)),
            dma((heads, 3, count)),
            dma((heads, 2, slabs)),
            dma((heads, slabs)),
            dma((heads, slabs)),
            dma((heads, 2, slabs)),
            dma((heads, slabs)),
            dma((heads, slabs)),
            dma((heads, count)),
            dma((heads, 4, count)),
            dma((heads, mp_count)),
            dma((heads, mp_count)),
            dma((count,)),
            dma((count,)),
            dma,
            dma((mp_count,)),
            dma((mp_count,)),
            dma((mp_count,)),
            dma,
        ],
        compiler_params=pltpu.CompilerParams(
            collective_id=0, has_side_effects=True, vmem_limit_bytes=VMEM_LIMIT
        ),
        cost_estimate=pl.CostEstimate(
            flops=5 * pairs * HD, bytes_accessed=total_rows * width * 8, transcendentals=pairs
        ),
        name="attention_backward",
    )(begin[None, :], weight, rotated_queries, output_grad, rotated_keys, values, pieces,
      value_weight)


def solution(mesh):
    placed = (
        P("ctx", None),
        P("ctx", "mp"),
        P("ctx", "mp"),
        P("ctx", "mp"),
        P(None, "mp"),
        P(),
        P(),
    )
    return jax.shard_map(
        on_device,
        mesh=mesh,
        in_specs=placed,
        out_specs=(P("ctx", "mp"), P("ctx", "mp"), P("ctx", "mp"), P("ctx", "mp")),
        check_vma=False,
    )
```

time: 573 us -> 159 us (0.28)
  waiting for transfers between devices: 419 us -> 0 us
  Pallas kernels: 0 us -> 142 us
  starting transfers between devices: 47 us -> 0 us
  local copies, waits for them, and re-layouts: 35.9 us -> 8.92 us
  other arithmetic: 27.3 us -> 2.39 us
  matrix products: 27.1 us -> 3.9 us
  between operations: 16.6 us -> 0.66 us
    ppermute x5 -> x0, waiting for transfers between devices: 229 us -> none  [from_partner(): return lax.ppermute(value, axis, pairs)]
    pallas_call x0 -> x1, Pallas kernels: none -> 142 us  [on_device(): pl.pallas_call(functools.partial(kernel, count, mp_count, heads, keep, x_...]
    reduce_scatter x2 -> x0, waiting for transfers between devices: 115 us -> none  [the longest x1 94.3 us: on_device(): lax.psum_scatter(lax.dot_general(sublayer_input, value_grad, (((0,), (0,)...]
    all_gather x2 -> x0, waiting for transfers between devices: 74 us -> none  [the longest x1 38.8 us: on_device(): lax.all_gather(rotated_keys, 'ctx', axis=0, tiled=True)]
    ppermute x5 -> x0, starting transfers between devices: 46.8 us -> none  [from_partner(): return lax.ppermute(value, axis, pairs)]
    dot_general x10 -> x1, matrix products: 27.1 us -> 3.9 us  [dot(): return jnp.dot(a, b, preferred_element_type=F32)]
    select_n x5 -> x1, other arithmetic: 10.2 us -> 0.01 us  [on_device(): weight = jnp.where(labelled, 4.0, 1.0).astype(F32)[:, None]]
    select_n x2 -> x1, local copies, waits for them, and re-layouts: 10.8 us -> 0.75 us  [on_device(): weight = jnp.where(labelled, 4.0, 1.0).astype(F32)[:, None]]
  transfers between devices with their start and end apart: 9 -> 0, of which waited for: 9 -> 0; matrix products, arithmetic and copies ran while one was open for 5% -> 0% of each run, Pallas kernels for 0% -> 0%
where the time goes in v1:
time: 159 us; the launch traced here: 158 us
  Pallas kernels  142 us (89%)
  local copies, waits for them, and re-layouts  8.92 us (6%)
  matrix products  3.9 us (2%)
  other arithmetic  2.39 us (2%)
    pallas_call x1, Pallas kernels, on_device(): pl.pallas_call(functools.partial(kernel, count, mp_count, heads, keep, x_...  142 us
    unnamed x4, local copies, waits for them, and re-layouts  7.4 us
    dot_general x1, matrix products, dot(): return jnp.dot(a, b, preferred_element_type=F32)  3.9 us

profile of v1, /device:TPU:0, one launch (start us, length us, event | category | flops | bytes accessed | tf_op | source)
XLA Modules:
  0.0 158.2 jit_solution(6836273049144223969)
XLA Ops:
  0.6 0.8 dynamic_slice.3
  1.4 1.6 convert_reduce_fusion
  3.0 0.8 compare_reduce_fusion
  3.8 0.7 copy.12.weight_ref
  4.6 3.9 %convolution_convert_fusion.v_ref = bf16[128,512]{1,0:T(8,128)(2,1)} fusion(bf16[128,4096]{1,0:T(8,128)(2,1)} %x_ref.1, bf16[4096,512]{1,0:T(8,128)(2,1)} %w_ref.1), kind=kOutput, calls=%fused_computation | convolution fusion | flops 536936448 | bytes 5373952 | tf_op jit(solution)/shard_map/dot_general | solution.py:44
  8.5 142.4 %attention_backward.1 = (bf16[128,4096]{1,0:T(8,128)(2,1)}, bf16[128,512]{1,0:T(8,128)(2,1)}, bf16[128,2048]{1,0:T(8,128)(2,1)}, bf16[256,512]{1,0:T(8,128)(2,1)}) custom-call(s32[1,128]{1,0:T(1,128)} %bitcast.5, f32[128,1]{1,0:T(8,128)} %copy.12.weight_ref, bf16[128,4096]{1,0:T(8,128)(2,1)} %q_ref.1, bf16[128,4096]{1,0:T(8,128)(2,1)} %g_ref.1, ...), custom_call_target="tpu_custom_call" | custom-call | flops 5368709120 | bytes 8388608 | tf_op jit(solution)/shard_map/attention_backward/pallas_call | solution.py:608
  150.8 2.3 %copy.17 = bf16[128,4096]{1,0:T(8,128)(2,1)} copy(bf16[128,4096]{1,0:T(8,128)(2,1)} %get-tuple-element.8) | data formatting | bytes 2097152
  153.1 1.6 copy.18
  154.7 1.9 %copy.19 = bf16[128,2048]{1,0:T(8,128)(2,1)} copy(bf16[128,2048]{1,0:T(8,128)(2,1)} %get-tuple-element.10) | data formatting | bytes 1048576
  156.6 1.7 %copy.20 = bf16[256,512]{1,0:T(8,128)(2,1)} copy(bf16[256,512]{1,0:T(8,128)(2,1)} %get-tuple-element.11) | data formatting | bytes 524288
  (2 shorter events, 0.0 us)

commit v2 on v1

--- a/solution.py
+++ b/solution.py
@@ -57,7 +57,7 @@
     for d in range(1, mp_count):
         peer = lax.rem(mine + d, mp_count)
         pl.semaphore_signal(barrier, inc=1, device_id={"mp": peer}, device_id_type=MESH)
-    pl.semaphore_wait(barrier, count - 1 + mp_count - 1)
+    return barrier
 
 
 def repeat(low, high, body):
@@ -70,13 +70,13 @@
 
 def kernel(
     count, mp_count, heads, keep, x_split,
-    begin_ref, weight_ref, q_ref, g_ref, k_ref, v_ref, x_ref, w_ref,
+    seg_ref, label_ref, q_ref, g_ref, k_ref, x_ref, w_ref,
     dq_ref, dk_ref, ig_ref, wg_ref,
     kv, part, rc, ry, rz, sy, sz, all_v, pair, xc, xt, wr,
     qs, qt, gs, gt, top, total, dotted, dq_acc, pb, sb, block_top, e_all, p_all, ig_acc,
-    g_recv, g_send, rc_sem, ry_sem, rz_sem, sc_sem, sy_sem, sz_sem,
-    ag_recv, ag_send, mp_recv, mp_send, x_recv, x_send, xf_recv, xf_send,
-    w_recv, w_send, w_own,
+    g_recv, g_send, gz_send, rc_sem, ry_sem, rz_sem, sc_sem, sy_sem, sz_sem,
+    ag_recv, ag_send, agz_send, mp_recv, mp_send, x_recv, x_send, xf_recv, xf_send,
+    w_recv, w_send,
 ):
     rows = q_ref.shape[0]
     wide = 2 * rows
@@ -89,10 +89,28 @@
     base = me - pos
     core_pos, side_pos = flip(pos, CORE), flip(pos, SIDE)
     both_pos = flip(side_pos, CORE)
-    last = slab == slabs - 1
     first_row = me * rows
     blocks = me // 2 + 1
-    greet(me, count, mp_count)
+    barrier = greet(me, count, mp_count)
+
+    if x_split:
+        values = jnp.zeros((rows, k_ref.shape[1]), F32)
+        for t in range(count):
+            values += dot(x_ref[t], w_ref[t * xc.shape[2]:(t + 1) * xc.shape[2], :])
+    else:
+        values = dot(x_ref[...], w_ref[...])
+    values = values.astype(BF)
+    position = first_row + lax.broadcasted_iota(jnp.int32, (rows, label_ref.shape[1]), 0)
+    loss_weight = jnp.max(
+        jnp.where(position == label_ref[...], 4.0, 1.0).astype(F32), axis=1, keepdims=True
+    )
+    segments = seg_ref[...]
+    own_segments = seg_ref[:, pl.ds(pl.multiple_of(first_row, rows), rows)]
+    begin = jnp.zeros((1, rows), jnp.int32)
+    for v in range(1, 4):
+        before = jnp.sum(jnp.where(segments < v, 1.0, 0.0), axis=1, keepdims=True)
+        begin = jnp.where(own_segments == v, before.astype(jnp.int32), begin)
+    pl.semaphore_wait(barrier, count - 1 + mp_count - 1)
 
     w_rows = w_ref.shape[0] // mp_count
 
@@ -101,62 +119,53 @@
         return remote(w_ref.at[at, :], wr.at[slot], w_send.at[peer], w_recv.at[slot], "mp", peer)
 
     def gather_copy(c, dest, block):
-        target = (me + SLAB, base + side_pos, base + core_pos)[dest]
+        target = (base + side_pos, base + core_pos)[dest]
         ref = kv.at[c, block]
         return remote(ref, ref, g_send.at[c, dest, block], g_recv.at[c, block], "ctx", target)
+
+    def gather_up(c, t):
+        ref = kv.at[c, me]
+        return remote(ref, ref, gz_send.at[c, t], g_recv.at[c, me], "ctx", t * SLAB + pos)
 
     def gather_own(c):
         cols = pl.ds(pl.multiple_of(c * HD, HD), HD)
         kv[c, me, :, :HD] = k_ref[:, cols]
-        kv[c, me, :, HD:] = v_ref[:, cols]
-
-        @pl.when(slab < slabs - 1)
-        def _():
-            gather_copy(c, 0, me).start()
-
+        repeat(slab + 1, slabs, lambda t: gather_up(c, t).start())
+        gather_copy(c, 0, me).start()
         gather_copy(c, 1, me).start()
-        gather_copy(c, 2, me).start()
 
     def gather_forward(c):
         def one(k):
             block = (slab - k) * SLAB + pos
             gather_copy(c, 0, block).wait_recv()
-
-            @pl.when(slab < slabs - 1)
-            def _():
-                gather_copy(c, 0, block).start()
-
+            gather_copy(c, 0, block).start()
             gather_copy(c, 1, block).start()
-            gather_copy(c, 2, block).start()
 
         repeat(1, slab + 1, one)
 
     def gather_cross(c):
         def one(k):
             block = (slab - k) * SLAB + side_pos
-            gather_copy(c, 1, block).wait_recv()
-            gather_copy(c, 2, block).start()
+            gather_copy(c, 0, block).wait_recv()
+            gather_copy(c, 1, block).start()
 
         repeat(0, slab + 1, one)
 
     def gather_arrive(c):
         def one(s):
-            gather_copy(c, 2, s * SLAB + core_pos).wait_recv()
-            gather_copy(c, 2, s * SLAB + both_pos).wait_recv()
+            gather_copy(c, 1, s * SLAB + core_pos).wait_recv()
+            gather_copy(c, 1, s * SLAB + both_pos).wait_recv()
 
         repeat(0, slab + 1, one)
 
     def gather_finish(c):
         def one(s):
-            @pl.when(slab < slabs - 1)
-            def _():
-                gather_copy(c, 0, s * SLAB + pos).wait_send()
-
+            gather_copy(c, 0, s * SLAB + pos).wait_send()
             gather_copy(c, 1, s * SLAB + pos).wait_send()
-            gather_copy(c, 2, s * SLAB + pos).wait_send()
-            gather_copy(c, 2, s * SLAB + side_pos).wait_send()
+            gather_copy(c, 1, s * SLAB + side_pos).wait_send()
 
         repeat(0, slab + 1, one)
+        repeat(slab + 1, slabs, lambda t: gather_up(c, t).wait_send())
 
     def core_copy(c, which, s):
         block = s * SLAB + (core_pos, both_pos)[which]
@@ -172,7 +181,13 @@
 
     def down_copy(c, s):
         return remote(
-            sz.at[c, s], rz.at[c, s], sz_sem.at[c, s], rz_sem.at[c, s], "ctx", me - SLAB
+            sz.at[c, s], rz.at[c, slab], sz_sem.at[c, s], rz_sem.at[c, slab],
+            "ctx", s * SLAB + pos,
+        )
+
+    def down_arrival(c, t):
+        return remote(
+            sz.at[c, t], rz.at[c, t], sz_sem.at[c, t], rz_sem.at[c, t], "ctx", base + core_pos
         )
 
     def reduce_core(c):
@@ -197,47 +212,27 @@
         side_copy(c, s).wait_recv()
         return both + ry[c, s].astype(F32)
 
-    def reduce_down(c):
-        def deliver(s, full):
-            @pl.when(s < slab)
-            def _():
-                sz[c, s] = full.astype(BF)
-                down_copy(c, s).start()
-
-            @pl.when(s == slab)
-            def _():
-                low = full.astype(BF)
-                dk_ref[:, pl.ds(pl.multiple_of(c * HD, HD), HD)] = low[:, :HD]
-                all_v[c, me] = low[:, HD:]
-                pair[mine, c] = low[:, HD:]
-
-        def one(s):
-            full = slab_total(c, s)
-
-            @pl.when(slab < slabs - 1)
-            def _():
-                down_copy(c, s).wait_recv()
-                deliver(s, full + rz[c, s].astype(F32))
-
-            @pl.when(last)
-            def _():
-                deliver(s, full)
-
-        repeat(0, slab + 1, one)
+    def reduce_send(c):
+        def one(s):
+            sz[c, s] = slab_total(c, s).astype(BF)
+            down_copy(c, s).start()
+
+        repeat(0, slab, one)
+
+    def reduce_final(c):
+        def one(t, full):
+            down_arrival(c, t).wait_recv()
+            return full + rz[c, t].astype(F32)
+
+        low = lax.fori_loop(slab + 1, slabs, one, slab_total(c, slab)).astype(BF)
+        dk_ref[:, pl.ds(pl.multiple_of(c * HD, HD), HD)] = low[:, :HD]
+        all_v[c, me] = low[:, HD:]
+        pair[mine, c] = low[:, HD:]
+        repeat(1, slabs, lambda k: spread_far(c, k).start())
+        spread_copy(c, 0, me).start()
+        spread_copy(c, 1, me).start()
         for d in range(1, mp_count):
-            peer = lax.rem(mine + d, mp_count)
-            pair_copy(c, peer, mine).start()
-
-        @pl.when(slab < slabs - 1)
-        def _():
-            spread_copy(c, 0, me).start()
-
-        @pl.when(slab > 0)
-        def _():
-            spread_copy(c, 1, me).start()
-
-        spread_copy(c, 2, me).start()
-        spread_copy(c, 3, me).start()
+            pair_copy(c, lax.rem(mine + d, mp_count), mine).start()
 
     def reduce_finish(c):
         def one(s):
@@ -258,72 +253,47 @@
         )
 
     def spread_copy(c, dest, block):
-        target = (me + SLAB, me - SLAB, base + side_pos, base + core_pos)[dest]
+        target = (base + side_pos, base + core_pos)[dest]
         ref = all_v.at[c, block]
         return remote(ref, ref, ag_send.at[c, dest, block], ag_recv.at[c, block], "ctx", target)
 
+    def spread_far(c, k):
+        t = lax.rem(slab + k, slabs)
+        ref = all_v.at[c, me]
+        return remote(ref, ref, agz_send.at[c, t], ag_recv.at[c, me], "ctx", t * SLAB + pos)
+
     def spread_forward(c):
         def one(k):
-            low, high = slab - k, slab + k
-
-            @pl.when(high < slabs)
-            def _():
-                block = high * SLAB + pos
-                spread_copy(c, 0, block).wait_recv()
-
-                @pl.when(slab > 0)
-                def _():
-                    spread_copy(c, 1, block).start()
-
-                spread_copy(c, 2, block).start()
-                spread_copy(c, 3, block).start()
-
-            @pl.when(low >= 0)
-            def _():
-                block = low * SLAB + pos
-                spread_copy(c, 0, block).wait_recv()
-
-                @pl.when(slab < slabs - 1)
-                def _():
-                    spread_copy(c, 0, block).start()
-
-                spread_copy(c, 2, block).start()
-                spread_copy(c, 3, block).start()
+            block = lax.rem(slab + k, slabs) * SLAB + pos
+            spread_copy(c, 0, block).wait_recv()
+            spread_copy(c, 0, block).start()
+            spread_copy(c, 1, block).start()
 
         repeat(1, slabs, one)
 
     def spread_cross(c):
-        def one(s):
-            block = s * SLAB + side_pos
-            spread_copy(c, 2, block).wait_recv()
-            spread_copy(c, 3, block).start()
+        def one(k):
+            block = lax.rem(slab + k, slabs) * SLAB + side_pos
+            spread_copy(c, 0, block).wait_recv()
+            spread_copy(c, 1, block).start()
 
         repeat(0, slabs, one)
 
     def spread_arrive(c):
         def one(s):
-            spread_copy(c, 3, s * SLAB + core_pos).wait_recv()
-            spread_copy(c, 3, s * SLAB + both_pos).wait_recv()
+            spread_copy(c, 1, s * SLAB + core_pos).wait_recv()
+            spread_copy(c, 1, s * SLAB + both_pos).wait_recv()
 
         repeat(0, slabs, one)
 
     def spread_finish(c):
         def one(s):
-            own = s * SLAB + pos
-
-            @pl.when((s <= slab) & (slab < slabs - 1))
-            def _():
-                spread_copy(c, 0, own).wait_send()
-
-            @pl.when((s >= slab) & (slab > 0))
-            def _():
-                spread_copy(c, 1, own).wait_send()
-
-            spread_copy(c, 2, own).wait_send()
-            spread_copy(c, 3, own).wait_send()
-            spread_copy(c, 3, s * SLAB + side_pos).wait_send()
+            spread_copy(c, 0, s * SLAB + pos).wait_send()
+            spread_copy(c, 1, s * SLAB + pos).wait_send()
+            spread_copy(c, 1, s * SLAB + side_pos).wait_send()
 
         repeat(0, slabs, one)
+        repeat(1, slabs, lambda k: spread_far(c, k).wait_send())
 
     owner = lax.rem(me, mp_count) == mine
     x_cols = xc.shape[2]
@@ -385,7 +355,6 @@
             for d in range(1, mp_count):
                 x_over(lax.rem(mine + d, mp_count)).wait_send()
 
-    begin = begin_ref[...]
     row_at = first_row + lax.broadcasted_iota(jnp.int32, (1, rows), 1)
 
     def visible(j):
@@ -408,7 +377,7 @@
             cols = pl.ds(pl.multiple_of((c * GROUP + g) * HD, HD), HD)
             span = slice(g * rows, (g + 1) * rows)
             q = q_ref[:, cols]
-            grad = (g_ref[:, cols].astype(F32) * weight_ref[...]).astype(BF)
+            grad = (g_ref[:, cols].astype(F32) * loss_weight).astype(BF)
             qs[span, :] = q
             gs[span, :] = grad
             qt[:, span] = q.T
@@ -473,12 +442,12 @@
             cols = pl.ds(pl.multiple_of((c * GROUP + g) * HD, HD), HD)
             dq_ref[:, cols] = (dq_acc[:, g * rows:(g + 1) * rows] * SCALE).T.astype(BF)
 
+    for c in range(heads):
+        kv[c, me, :, HD:] = values[:, c * HD:(c + 1) * HD]
     repeat(0, heads, gather_own)
     for d in range(1, mp_count):
         weight_copy(lax.rem(mine + d, mp_count), mine).start()
-    own_rows = pl.ds(pl.multiple_of(mine * w_rows, w_rows), w_rows)
-    own_weight = pltpu.make_async_copy(w_ref.at[own_rows, :], wr.at[mine], w_own)
-    own_weight.start()
+
     early = slab < slabs // 2
     ahead = jnp.where(early, heads, 1)
 
@@ -506,6 +475,10 @@
         def _():
             reduce_side(c - 1)
 
+        @pl.when(c > 1)
+        def _():
+            reduce_final(c - 2)
+
         second_pass(c)
         reduce_core(c)
 
@@ -515,26 +488,25 @@
 
         @pl.when(c > 0)
         def _():
-            reduce_down(c - 1)
-
-        @pl.when(c > 1)
-        def _():
-            spread_forward(c - 2)
+            reduce_send(c - 1)
 
     repeat(0, heads, head)
     final = heads - 1
     reduce_side(final)
+    if heads > 1:
+        reduce_final(final - 1)
+    repeat(0, final - 1, spread_forward)
+    reduce_send(final)
     x_forward()
-    reduce_down(final)
     if heads > 1:
-        spread_forward(heads - 2)
-    spread_forward(final)
-
-    repeat(0, heads, spread_cross)
+        spread_forward(final - 1)
+    reduce_final(final)
+    repeat(0, final, spread_cross)
+
     x_arrive()
     for i in range(count):
         xt[:, i * rows:(i + 1) * rows] = xc[i].T
-    own_weight.wait()
+    spread_forward(final)
     for d in range(1, mp_count):
         peer = lax.rem(mine + d, mp_count)
         weight_copy(peer, peer).wait_recv()
@@ -543,16 +515,19 @@
 
     contract = (((1,), (1,)), ((), ()))
 
-    def input_term(m):
+    def input_term(c, m, block):
+        return lax.dot_general(pair[m, c], block, contract, preferred_element_type=F32)
+
+    own_rows = pl.ds(pl.multiple_of(mine * w_rows, w_rows), w_rows)
+    for c in range(heads):
+        cols = slice(c * HD, (c + 1) * HD)
+        term = input_term(c, mine, w_ref[own_rows, cols])
+        ig_acc[...] = term if c == 0 else ig_acc[...] + term
+    spread_cross(final)
+    for d in range(1, mp_count):
+        peer = lax.rem(mine + d, mp_count)
         for c in range(heads):
-            term = lax.dot_general(
-                pair[m, c], wr[m, :, c * HD:(c + 1) * HD], contract,
-                preferred_element_type=F32,
-            )
-            ig_acc[...] += term
-
-    ig_acc[...] = jnp.zeros_like(ig_acc)
-    repeat(0, mp_count, input_term)
+            ig_acc[...] += input_term(c, peer, wr[peer, :, c * HD:(c + 1) * HD])
     ig_ref[...] = ig_acc[...].astype(BF)
     for c in range(heads):
         spread_arrive(c)
@@ -569,6 +544,11 @@
     repeat(0, heads, gather_finish)
     repeat(0, heads, reduce_finish)
     repeat(0, heads, spread_finish)
+
+
+def hand_over(*refs):
+    for i in range(4):
+        refs[4 + i][...] = refs[i][...]
 
 
 def on_device(
@@ -584,15 +564,6 @@
     heads = width // HD
     span = GROUP * rows
     kb = 2 * rows
-    first_row = lax.axis_index("ctx") * rows
-    own = first_row + jnp.arange(rows, dtype=jnp.int32)
-    labelled = jnp.any(own[:, None] == label_positions[None, :], axis=1)
-    weight = jnp.where(labelled, 4.0, 1.0).astype(F32)[:, None]
-    own_segments = lax.dynamic_slice_in_dim(segment_ids, first_row, rows)
-    begin = jnp.sum(
-        (segment_ids[:, None] < own_segments[None, :]).astype(jnp.int32), axis=0, dtype=jnp.int32
-    )
-    values = dot(sublayer_input, value_weight).astype(BF)
     x_cols = features // count
     x_split = x_cols % 128 != 0
     pieces = sublayer_input
@@ -601,11 +572,10 @@
     keep = total_rows <= 4096
     kept = (total_rows // kb, kb, span) if keep else (1, 8, 128)
     vmem = pl.BlockSpec(memory_space=pltpu.VMEM)
-    anywhere = pl.BlockSpec(memory_space=pl.ANY)
     dma = pltpu.SemaphoreType.DMA
     chunk = (rows, 2 * HD)
     pairs = rows * GROUP * heads * total_rows
-    return pl.pallas_call(
+    results = pl.pallas_call(
         functools.partial(kernel, count, mp_count, heads, keep, x_split),
         out_shape=(
             jax.ShapeDtypeStruct(rotated_queries.shape, BF),
@@ -613,7 +583,7 @@
             jax.ShapeDtypeStruct((rows, features // mp_count), BF),
             jax.ShapeDtypeStruct((x_cols, width), BF),
         ),
-        in_specs=[vmem] * 7 + [anywhere],
+        in_specs=[vmem] * 7,
         out_specs=(vmem,) * 4,
         scratch_shapes=[
             pltpu.VMEM((heads, count) + chunk, BF),
@@ -643,7 +613,8 @@
             pltpu.VMEM(kept, F32),
             pltpu.VMEM((rows, features // mp_count), F32),
             dma((heads, count)),
-            dma((heads, 3, count)),
+            dma((heads, 2, count)),
+            dma((heads, slabs)),
             dma((heads, 2, slabs)),
             dma((heads, slabs)),
             dma((heads, slabs)),
@@ -651,7 +622,8 @@
             dma((heads, slabs)),
             dma((heads, slabs)),
             dma((heads, count)),
-            dma((heads, 4, count)),
+            dma((heads, 2, count)),
+            dma((heads, slabs)),
             dma((heads, mp_count)),
             dma((heads, mp_count)),
             dma((count,)),
@@ -660,7 +632,6 @@
             dma((mp_count,)),
             dma((mp_count,)),
             dma((mp_count,)),
-            dma,
         ],
         compiler_params=pltpu.CompilerParams(
             collective_id=0, has_side_effects=True, vmem_limit_bytes=VMEM_LIMIT
@@ -669,8 +640,15 @@
             flops=5 * pairs * HD, bytes_accessed=total_rows * width * 8, transcendentals=pairs
         ),
         name="attention_backward",
-    )(begin[None, :], weight, rotated_queries, output_grad, rotated_keys, values, pieces,
-      value_weight)
+    )(segment_ids[None, :], label_positions[None, :], rotated_queries, output_grad,
+      rotated_keys, pieces, value_weight)
+    return pl.pallas_call(
+        hand_over,
+        out_shape=tuple(jax.ShapeDtypeStruct(r.shape, r.dtype) for r in results),
+        in_specs=[vmem] * 4,
+        out_specs=(vmem,) * 4,
+        name="hand_over",
+    )(*results)
 
 
 def solution(mesh):

time: 159 us -> 112 us (0.70)
  Pallas kernels: 142 us -> 110 us
  local copies, waits for them, and re-layouts: 8.92 us -> 0 us
  matrix products: 3.9 us -> 0 us
  other arithmetic: 2.39 us -> 0 us
    pallas_call x1, Pallas kernels: 142 us -> 107 us  [on_device(): pl.pallas_call(functools.partial(kernel, count, mp_count, heads, keep, x_...]
    unnamed x4 -> x0, local copies, waits for them, and re-layouts: 7.4 us -> none
    dot_general x1 -> x0, matrix products: 3.9 us -> none  [dot(): return jnp.dot(a, b, preferred_element_type=F32)]
    pallas_call x0 -> x1, Pallas kernels: none -> 2.8 us  [on_device(): pl.pallas_call(hand_over, out_shape=tuple((jax.ShapeDtypeStruct(r.shape,...]
where the time goes in v2:
time: 112 us; the launch traced here: 111 us
  Pallas kernels  110 us (98%)
    pallas_call x1, Pallas kernels, on_device(): pl.pallas_call(functools.partial(kernel, count, mp_count, heads, keep, x_...  107 us
    pallas_call x1, Pallas kernels, on_device(): pl.pallas_call(hand_over, out_shape=tuple((jax.ShapeDtypeStruct(r.shape,...  2.8 us

profile of v2, /device:TPU:0, one launch (start us, length us, event | category | flops | bytes accessed | tf_op | source)
XLA Modules:
  0.0 110.5 jit_solution(6428408496266431703)
XLA Ops:
  0.6 107.1 %attention_backward.1 = (bf16[128,4096]{1,0:T(8,128)(2,1)}, bf16[128,512]{1,0:T(8,128)(2,1)}, bf16[128,2048]{1,0:T(8,128)(2,1)}, bf16[256,512]{1,0:T(8,128)(2,1)}) custom-call(s32[1,2048]{1,0:T(1,128)} %bitcast.2, s32[1,128]{1,0:T(1,128)} %bitcast.3, bf16[128,4096]{1,0:T(8,128)(2,1)} %q_ref.1, bf16[128,4096]{1,0:T(8,128)(2,1)} %g_ref.1, ...), custom_call_target="tpu_custom_call" | custom-call | flops 5368709120 | bytes 8388608 | tf_op jit(solution)/shard_map/attention_backward/pallas_call | solution.py:578
  107.7 2.8 %hand_over.1 = (bf16[128,4096]{1,0:T(8,128)(2,1)}, bf16[128,512]{1,0:T(8,128)(2,1)}, bf16[128,2048]{1,0:T(8,128)(2,1)}, bf16[256,512]{1,0:T(8,128)(2,1)}) custom-call(bf16[128,4096]{1,0:T(8,128)(2,1)} %get-tuple-element.8.refs_0_, bf16[128,512]{1,0:T(8,128)(2,1)} %get-tuple-element.9.refs_1_, bf16[128,2048]{1,0:T(8,128)(2,1)} %get-tuple-element.10.refs_2_, ...), custom_call_target="tpu_custom_call" | custom-call | tf_op jit(solution)/shard_map/hand_over/pallas_call | solution.py:645

commit v3 on v2

--- a/solution.py
+++ b/solution.py
@@ -444,18 +444,25 @@
 
     for c in range(heads):
         kv[c, me, :, HD:] = values[:, c * HD:(c + 1) * HD]
-    repeat(0, heads, gather_own)
+    early = slab < slabs // 2
+    gather_own(0)
+    gather_forward(0)
+    gather_cross(0)
     for d in range(1, mp_count):
         weight_copy(lax.rem(mine + d, mp_count), mine).start()
-
-    early = slab < slabs // 2
-    ahead = jnp.where(early, heads, 1)
-
-    def gather_both(c):
+    if heads > 1:
+        gather_own(1)
+
+    def gather_early(c):
         gather_forward(c)
+
+        @pl.when(c < heads - 1)
+        def _():
+            gather_own(c + 1)
+
         gather_cross(c)
 
-    repeat(0, ahead, gather_both)
+    repeat(1, jnp.where(early, heads, 1), gather_early)
 
     def head(c):
         prepare(c)
@@ -471,6 +478,10 @@
         def _():
             gather_forward(c + 1)
 
+            @pl.when(c < heads - 2)
+            def _():
+                gather_own(c + 2)
+
         @pl.when(c > 0)
         def _():
             reduce_side(c - 1)
@@ -478,6 +489,10 @@
         @pl.when(c > 1)
         def _():
             reduce_final(c - 2)
+
+        @pl.when(c == heads - 1)
+        def _():
+            x_forward()
 
         second_pass(c)
         reduce_core(c)
@@ -489,51 +504,62 @@
         @pl.when(c > 0)
         def _():
             reduce_send(c - 1)
+
+        @pl.when(c > 1)
+        def _():
+            spread_forward(c - 2)
 
     repeat(0, heads, head)
     final = heads - 1
     reduce_side(final)
     if heads > 1:
         reduce_final(final - 1)
-    repeat(0, final - 1, spread_forward)
+    repeat(0, final - 1, spread_cross)
     reduce_send(final)
-    x_forward()
     if heads > 1:
         spread_forward(final - 1)
-    reduce_final(final)
-    repeat(0, final, spread_cross)
-
-    x_arrive()
-    for i in range(count):
-        xt[:, i * rows:(i + 1) * rows] = xc[i].T
-    spread_forward(final)
-    for d in range(1, mp_count):
-        peer = lax.rem(mine + d, mp_count)
-        weight_copy(peer, peer).wait_recv()
-        for c in range(heads):
+
+    contract = (((1,), (1,)), ((), ()))
+    own_rows = pl.ds(pl.multiple_of(mine * w_rows, w_rows), w_rows)
+
+    def input_terms(c):
+        cols = slice(c * HD, (c + 1) * HD)
+
+        def term(m, block):
+            return lax.dot_general(pair[m, c], block, contract, preferred_element_type=F32)
+
+        found = term(mine, w_ref[own_rows, cols])
+        ig_acc[...] = found if c == 0 else ig_acc[...] + found
+        for d in range(1, mp_count):
+            peer = lax.rem(mine + d, mp_count)
             pair_copy(c, peer, peer).wait_recv()
-
-    contract = (((1,), (1,)), ((), ()))
-
-    def input_term(c, m, block):
-        return lax.dot_general(pair[m, c], block, contract, preferred_element_type=F32)
-
-    own_rows = pl.ds(pl.multiple_of(mine * w_rows, w_rows), w_rows)
-    for c in range(heads):
-        cols = slice(c * HD, (c + 1) * HD)
-        term = input_term(c, mine, w_ref[own_rows, cols])
-        ig_acc[...] = term if c == 0 else ig_acc[...] + term
-    spread_cross(final)
-    for d in range(1, mp_count):
-        peer = lax.rem(mine + d, mp_count)
-        for c in range(heads):
-            ig_acc[...] += input_term(c, peer, wr[peer, :, c * HD:(c + 1) * HD])
-    ig_ref[...] = ig_acc[...].astype(BF)
-    for c in range(heads):
+            ig_acc[...] += term(peer, wr[peer, :, cols])
+
+    def weight_term(c):
         spread_arrive(c)
         wg_ref[:, c * HD:(c + 1) * HD] = dot(
             xt[...], all_v[c].reshape(count * rows, HD)
         ).astype(BF)
+
+    x_arrive()
+    for i in range(count):
+        xt[:, i * rows:(i + 1) * rows] = xc[i].T
+    for d in range(1, mp_count):
+        peer = lax.rem(mine + d, mp_count)
+        weight_copy(peer, peer).wait_recv()
+    for c in range(final - 1):
+        weight_term(c)
+    reduce_final(final)
+    if heads > 1:
+        spread_cross(final - 1)
+    for c in range(final):
+        input_terms(c)
+    spread_forward(final)
+    input_terms(final)
+    spread_cross(final)
+    ig_ref[...] = ig_acc[...].astype(BF)
+    for c in range(max(final - 1, 0), heads):
+        weight_term(c)
 
     for d in range(1, mp_count):
         peer = lax.rem(mine + d, mp_count)

time: 112 us -> 111 us (level)
  no operation moved by 1% of the time
where the time goes in v3:
time: 111 us
  Pallas kernels  110 us (99%)
    pallas_call x1, Pallas kernels, on_device(): pl.pallas_call(functools.partial(kernel, count, mp_count, heads, keep, x_...  107 us
    pallas_call x1, Pallas kernels, on_device(): pl.pallas_call(hand_over, out_shape=tuple((jax.ShapeDtypeStruct(r.shape,...  2.8 us

profile of v3, /device:TPU:0, one launch (start us, length us, event | category | flops | bytes accessed | tf_op | source)
XLA Modules:
  0.0 110.5 jit_solution(13185467647517614717)
XLA Ops:
  0.6 107.1 %attention_backward.1 = (bf16[128,4096]{1,0:T(8,128)(2,1)}, bf16[128,512]{1,0:T(8,128)(2,1)}, bf16[128,2048]{1,0:T(8,128)(2,1)}, bf16[256,512]{1,0:T(8,128)(2,1)}) custom-call(s32[1,2048]{1,0:T(1,128)} %bitcast.2, s32[1,128]{1,0:T(1,128)} %bitcast.3, bf16[128,4096]{1,0:T(8,128)(2,1)} %q_ref.1, bf16[128,4096]{1,0:T(8,128)(2,1)} %g_ref.1, ...), custom_call_target="tpu_custom_call" | custom-call | flops 5368709120 | bytes 8388608 | tf_op jit(solution)/shard_map/attention_backward/pallas_call | solution.py:604
  107.7 2.8 %hand_over.1 = (bf16[128,4096]{1,0:T(8,128)(2,1)}, bf16[128,512]{1,0:T(8,128)(2,1)}, bf16[128,2048]{1,0:T(8,128)(2,1)}, bf16[256,512]{1,0:T(8,128)(2,1)}) custom-call(bf16[128,4096]{1,0:T(8,128)(2,1)} %get-tuple-element.8.refs_0_, bf16[128,512]{1,0:T(8,128)(2,1)} %get-tuple-element.9.refs_1_, bf16[128,2048]{1,0:T(8,128)(2,1)} %get-tuple-element.10.refs_2_, ...), custom_call_target="tpu_custom_call" | custom-call | tf_op jit(solution)/shard_map/hand_over/pallas_call | solution.py:671

commit v4 on v3

--- a/solution.py
+++ b/solution.py
@@ -74,8 +74,8 @@
     dq_ref, dk_ref, ig_ref, wg_ref,
     kv, part, rc, ry, rz, sy, sz, all_v, pair, xc, xt, wr,
     qs, qt, gs, gt, top, total, dotted, dq_acc, pb, sb, block_top, e_all, p_all, ig_acc,
-    g_recv, g_send, gz_send, rc_sem, ry_sem, rz_sem, sc_sem, sy_sem, sz_sem,
-    ag_recv, ag_send, agz_send, mp_recv, mp_send, x_recv, x_send, xf_recv, xf_send,
+    gz_recv, gz_send, gy_sem, gc_sem, rc_sem, ry_sem, rz_sem, sz_sem,
+    az_recv, az_send, ay_sem, ac_sem, mp_recv, mp_send, x_recv, x_send, xf_recv, xf_send,
     w_recv, w_send,
 ):
     rows = q_ref.shape[0]
@@ -87,8 +87,8 @@
     slab = me // SLAB
     pos = lax.rem(me, SLAB)
     base = me - pos
-    core_pos, side_pos = flip(pos, CORE), flip(pos, SIDE)
-    both_pos = flip(side_pos, CORE)
+    core, side = lax.rem(pos, 2), pos // 2
+    core_mate, side_mate = base + flip(pos, CORE), base + flip(pos, SIDE)
     first_row = me * rows
     blocks = me // 2 + 1
     barrier = greet(me, count, mp_count)
@@ -118,65 +118,53 @@
         at = pl.ds(pl.multiple_of(peer * w_rows, w_rows), w_rows)
         return remote(w_ref.at[at, :], wr.at[slot], w_send.at[peer], w_recv.at[slot], "mp", peer)
 
-    def gather_copy(c, dest, block):
-        target = (base + side_pos, base + core_pos)[dest]
-        ref = kv.at[c, block]
-        return remote(ref, ref, g_send.at[c, dest, block], g_recv.at[c, block], "ctx", target)
-
     def gather_up(c, t):
-        ref = kv.at[c, me]
-        return remote(ref, ref, gz_send.at[c, t], g_recv.at[c, me], "ctx", t * SLAB + pos)
+        ref = kv.at[c, core, side, slab]
+        return remote(
+            ref, ref, gz_send.at[c, t], gz_recv.at[c, slab], "ctx", t * SLAB + pos
+        )
+
+    def gather_below(c, t):
+        ref = kv.at[c, core, side, t]
+        return remote(ref, ref, gz_send.at[c, t], gz_recv.at[c, t], "ctx", core_mate)
+
+    def gather_side(c, column):
+        ref = kv.at[c, core, column]
+        return remote(ref, ref, gy_sem.at[c, 0], gy_sem.at[c, 1], "ctx", side_mate)
+
+    def gather_core(c, half):
+        ref = kv.at[c, half]
+        return remote(ref, ref, gc_sem.at[c, 0], gc_sem.at[c, 1], "ctx", core_mate)
 
     def gather_own(c):
         cols = pl.ds(pl.multiple_of(c * HD, HD), HD)
-        kv[c, me, :, :HD] = k_ref[:, cols]
+        kv[c, core, side, slab, :, :HD] = k_ref[:, cols]
         repeat(slab + 1, slabs, lambda t: gather_up(c, t).start())
-        gather_copy(c, 0, me).start()
-        gather_copy(c, 1, me).start()
 
     def gather_forward(c):
-        def one(k):
-            block = (slab - k) * SLAB + pos
-            gather_copy(c, 0, block).wait_recv()
-            gather_copy(c, 0, block).start()
-            gather_copy(c, 1, block).start()
-
-        repeat(1, slab + 1, one)
+        repeat(0, slab, lambda t: gather_below(c, t).wait_recv())
+        gather_side(c, side).start()
 
     def gather_cross(c):
-        def one(k):
-            block = (slab - k) * SLAB + side_pos
-            gather_copy(c, 0, block).wait_recv()
-            gather_copy(c, 1, block).start()
-
-        repeat(0, slab + 1, one)
+        gather_side(c, 1 - side).wait_recv()
+        gather_core(c, core).start()
 
     def gather_arrive(c):
-        def one(s):
-            gather_copy(c, 1, s * SLAB + core_pos).wait_recv()
-            gather_copy(c, 1, s * SLAB + both_pos).wait_recv()
-
-        repeat(0, slab + 1, one)
+        gather_core(c, 1 - core).wait_recv()
 
     def gather_finish(c):
-        def one(s):
-            gather_copy(c, 0, s * SLAB + pos).wait_send()
-            gather_copy(c, 1, s * SLAB + pos).wait_send()
-            gather_copy(c, 1, s * SLAB + side_pos).wait_send()
-
-        repeat(0, slab + 1, one)
+        gather_side(c, side).wait_send()
+        gather_core(c, core).wait_send()
         repeat(slab + 1, slabs, lambda t: gather_up(c, t).wait_send())
 
-    def core_copy(c, which, s):
-        block = s * SLAB + (core_pos, both_pos)[which]
+    def core_copy(c):
         return remote(
-            part.at[c, block], rc.at[c, which, s],
-            sc_sem.at[c, which, s], rc_sem.at[c, which, s], "ctx", base + core_pos,
+            part.at[c, 1 - core], rc.at[c], rc_sem.at[c, 0], rc_sem.at[c, 1], "ctx", core_mate
         )
 
-    def side_copy(c, s):
+    def side_copy(c):
         return remote(
-            sy.at[c, s], ry.at[c, s], sy_sem.at[c, s], ry_sem.at[c, s], "ctx", base + side_pos
+            sy.at[c], ry.at[c], ry_sem.at[c, 0], ry_sem.at[c, 1], "ctx", side_mate
         )
 
     def down_copy(c, s):
@@ -187,32 +175,29 @@
 
     def down_arrival(c, t):
         return remote(
-            sz.at[c, t], rz.at[c, t], sz_sem.at[c, t], rz_sem.at[c, t], "ctx", base + core_pos
+            sz.at[c, t], rz.at[c, t], sz_sem.at[c, t], rz_sem.at[c, t], "ctx", core_mate
         )
 
     def reduce_core(c):
+        core_copy(c).start()
+
+    def reduce_side(c):
+        core_copy(c).wait_recv()
+
         def one(s):
-            core_copy(c, 1, s).start()
-            core_copy(c, 0, s).start()
+            both = part[c, core, 1 - side, s].astype(F32) + rc[c, 1 - side, s].astype(F32)
+            sy[c, s] = both.astype(BF)
 
         repeat(0, slab + 1, one)
-
-    def reduce_side(c):
-        def one(s):
-            core_copy(c, 1, s).wait_recv()
-            both = part[c, s * SLAB + side_pos].astype(F32) + rc[c, 1, s].astype(F32)
-            sy[c, s] = both.astype(BF)
-            side_copy(c, s).start()
-
-        repeat(0, slab + 1, one)
+        side_copy(c).start()
 
     def slab_total(c, s):
-        core_copy(c, 0, s).wait_recv()
-        both = part[c, s * SLAB + pos].astype(F32) + rc[c, 0, s].astype(F32)
-        side_copy(c, s).wait_recv()
+        both = part[c, core, side, s].astype(F32) + rc[c, side, s].astype(F32)
         return both + ry[c, s].astype(F32)
 
     def reduce_send(c):
+        side_copy(c).wait_recv()
+
         def one(s):
             sz[c, s] = slab_total(c, s).astype(BF)
             down_copy(c, s).start()
@@ -226,73 +211,57 @@
 
         low = lax.fori_loop(slab + 1, slabs, one, slab_total(c, slab)).astype(BF)
         dk_ref[:, pl.ds(pl.multiple_of(c * HD, HD), HD)] = low[:, :HD]
-        all_v[c, me] = low[:, HD:]
+        all_v[c, core, side, slab] = low[:, HD:]
         pair[mine, c] = low[:, HD:]
         repeat(1, slabs, lambda k: spread_far(c, k).start())
-        spread_copy(c, 0, me).start()
-        spread_copy(c, 1, me).start()
         for d in range(1, mp_count):
             pair_copy(c, lax.rem(mine + d, mp_count), mine).start()
 
     def reduce_finish(c):
-        def one(s):
-            core_copy(c, 0, s).wait_send()
-            core_copy(c, 1, s).wait_send()
-            side_copy(c, s).wait_send()
-
-            @pl.when(s < slab)
-            def _():
-                down_copy(c, s).wait_send()
-
-        repeat(0, slab + 1, one)
+        core_copy(c).wait_send()
+        side_copy(c).wait_send()
+        repeat(0, slab, lambda t: down_copy(c, t).wait_send())
 
     def pair_copy(c, peer, slot):
         return remote(
-            all_v.at[c, me], pair.at[slot, c], mp_send.at[c, peer], mp_recv.at[c, slot],
+            all_v.at[c, core, side, slab], pair.at[slot, c], mp_send.at[c, peer], mp_recv.at[c, slot],
             "mp", peer,
         )
 
-    def spread_copy(c, dest, block):
-        target = (base + side_pos, base + core_pos)[dest]
-        ref = all_v.at[c, block]
-        return remote(ref, ref, ag_send.at[c, dest, block], ag_recv.at[c, block], "ctx", target)
-
     def spread_far(c, k):
         t = lax.rem(slab + k, slabs)
-        ref = all_v.at[c, me]
-        return remote(ref, ref, agz_send.at[c, t], ag_recv.at[c, me], "ctx", t * SLAB + pos)
+        ref = all_v.at[c, core, side, slab]
+        return remote(
+            ref, ref, az_send.at[c, t], az_recv.at[c, slab], "ctx", t * SLAB + pos
+        )
+
+    def spread_near(c, k):
+        t = lax.rem(slab + k, slabs)
+        ref = all_v.at[c, core, side, t]
+        return remote(ref, ref, az_send.at[c, t], az_recv.at[c, t], "ctx", core_mate)
+
+    def spread_side(c, column):
+        ref = all_v.at[c, core, column]
+        return remote(ref, ref, ay_sem.at[c, 0], ay_sem.at[c, 1], "ctx", side_mate)
+
+    def spread_core(c, half):
+        ref = all_v.at[c, half]
+        return remote(ref, ref, ac_sem.at[c, 0], ac_sem.at[c, 1], "ctx", core_mate)
 
     def spread_forward(c):
-        def one(k):
-            block = lax.rem(slab + k, slabs) * SLAB + pos
-            spread_copy(c, 0, block).wait_recv()
-            spread_copy(c, 0, block).start()
-            spread_copy(c, 1, block).start()
-
-        repeat(1, slabs, one)
+        repeat(1, slabs, lambda k: spread_near(c, k).wait_recv())
+        spread_side(c, side).start()
 
     def spread_cross(c):
-        def one(k):
-            block = lax.rem(slab + k, slabs) * SLAB + side_pos
-            spread_copy(c, 0, block).wait_recv()
-            spread_copy(c, 1, block).start()
-
-        repeat(0, slabs, one)
+        spread_side(c, 1 - side).wait_recv()
+        spread_core(c, core).start()
 
     def spread_arrive(c):
-        def one(s):
-            spread_copy(c, 1, s * SLAB + core_pos).wait_recv()
-            spread_copy(c, 1, s * SLAB + both_pos).wait_recv()
-
-        repeat(0, slabs, one)
+        spread_core(c, 1 - core).wait_recv()
 
     def spread_finish(c):
-        def one(s):
-            spread_copy(c, 0, s * SLAB + pos).wait_send()
-            spread_copy(c, 1, s * SLAB + pos).wait_send()
-            spread_copy(c, 1, s * SLAB + side_pos).wait_send()
-
-        repeat(0, slabs, one)
+        spread_side(c, side).wait_send()
+        spread_core(c, core).wait_send()
         repeat(1, slabs, lambda k: spread_far(c, k).wait_send())
 
     owner = lax.rem(me, mp_count) == mine
@@ -363,10 +332,10 @@
         return jnp.concatenate([seen, seen], axis=1)
 
     def key_block(c, j):
-        return kv[c, pl.ds(2 * j, 2), :, :HD].reshape(kb, HD)
+        return kv[c, :, lax.rem(j, 2), j // 2, :, :HD].reshape(kb, HD)
 
     def value_block(c, j):
-        return kv[c, pl.ds(2 * j, 2), :, HD:].reshape(kb, HD)
+        return kv[c, :, lax.rem(j, 2), j // 2, :, HD:].reshape(kb, HD)
 
     def terms(c, j, seen, span):
         scores = dot(key_block(c, j), qt[:, span]) * (SCALE * LOG2E)
@@ -413,7 +382,7 @@
 
     def second_pass(c):
         for i in range(SLAB):
-            part[c, base + i] = jnp.zeros((rows, 2 * HD), BF)
+            part[c, i // 2, i % 2, slab] = jnp.zeros((rows, 2 * HD), BF)
 
         def one(j):
             if not keep:
@@ -430,11 +399,11 @@
                 pb[:, span] = probs.astype(BF)
                 sb[:, span] = (probs * (grad_probs - dotted[:, span])).astype(BF)
             low = sb[...]
-            at = pl.ds(2 * j, 2)
+            column, at = lax.rem(j, 2), j // 2
             value_term = dot(pb[...], gs[...]).astype(BF)
             key_term = (dot(low, qs[...]) * SCALE).astype(BF)
-            part[c, at, :, HD:] = value_term.reshape(2, rows, HD)
-            part[c, at, :, :HD] = key_term.reshape(2, rows, HD)
+            part[c, :, column, at, :, HD:] = value_term.reshape(2, rows, HD)
+            part[c, :, column, at, :, :HD] = key_term.reshape(2, rows, HD)
             dq_acc[...] += dot(key_block(c, j).T, low)
 
         repeat(0, blocks, one)
@@ -443,7 +412,7 @@
             dq_ref[:, cols] = (dq_acc[:, g * rows:(g + 1) * rows] * SCALE).T.astype(BF)
 
     for c in range(heads):
-        kv[c, me, :, HD:] = values[:, c * HD:(c + 1) * HD]
+        kv[c, core, side, slab, :, HD:] = values[:, c * HD:(c + 1) * HD]
     early = slab < slabs // 2
     gather_own(0)
     gather_forward(0)
@@ -543,7 +512,8 @@
 
     x_arrive()
     for i in range(count):
-        xt[:, i * rows:(i + 1) * rows] = xc[i].T
+        at = (i % 2 * 2 + i % SLAB // 2) * slabs + i // SLAB
+        xt[:, at * rows:(at + 1) * rows] = xc[i].T
     for d in range(1, mp_count):
         peer = lax.rem(mine + d, mp_count)
         weight_copy(peer, peer).wait_recv()
@@ -612,14 +582,14 @@
         in_specs=[vmem] * 7,
         out_specs=(vmem,) * 4,
         scratch_shapes=[
-            pltpu.VMEM((heads, count) + chunk, BF),
-            pltpu.VMEM((heads, count) + chunk, BF),
+            pltpu.VMEM((heads, 2, 2, slabs) + chunk, BF),
+            pltpu.VMEM((heads, 2, 2, slabs) + chunk, BF),
             pltpu.VMEM((heads, 2, slabs) + chunk, BF),
             pltpu.VMEM((heads, slabs) + chunk, BF),
             pltpu.VMEM((heads, slabs) + chunk, BF),
             pltpu.VMEM((heads, slabs) + chunk, BF),
             pltpu.VMEM((heads, slabs) + chunk, BF),
-            pltpu.VMEM((heads, count, rows, HD), BF),
+            pltpu.VMEM((heads, 2, 2, slabs, rows, HD), BF),
             pltpu.VMEM((mp_count, heads, rows, HD), BF),
             pltpu.VMEM((count, rows, x_cols), BF),
             pltpu.VMEM((x_cols, total_rows), BF),
@@ -638,18 +608,18 @@
             pltpu.VMEM(kept, F32),
             pltpu.VMEM(kept, F32),
             pltpu.VMEM((rows, features // mp_count), F32),
-            dma((heads, count)),
-            dma((heads, 2, count)),
-            dma((heads, slabs)),
-            dma((heads, 2, slabs)),
             dma((heads, slabs)),
             dma((heads, slabs)),
-            dma((heads, 2, slabs)),
+            dma((heads, 2)),
+            dma((heads, 2)),
+            dma((heads, 2)),
+            dma((heads, 2)),
             dma((heads, slabs)),
             dma((heads, slabs)),
-            dma((heads, count)),
-            dma((heads, 2, count)),
             dma((heads, slabs)),
+            dma((heads, slabs)),
+            dma((heads, 2)),
+            dma((heads, 2)),
             dma((heads, mp_count)),
             dma((heads, mp_count)),
             dma((count,)),

time: 111 us -> 122 us (1.099)
  Pallas kernels: 110 us -> 121 us
    pallas_call x1, Pallas kernels: 107 us -> 118 us  [on_device(): pl.pallas_call(functools.partial(kernel, count, mp_count, heads, keep, x_...]
where the time goes in v4:
time: 122 us
  Pallas kernels  121 us (99%)
    pallas_call x1, Pallas kernels, on_device(): pl.pallas_call(functools.partial(kernel, count, mp_count, heads, keep, x_...  118 us
    pallas_call x1, Pallas kernels, on_device(): pl.pallas_call(hand_over, out_shape=tuple((jax.ShapeDtypeStruct(r.shape,...  2.8 us

profile of v4, /device:TPU:0, one launch (start us, length us, event | category | flops | bytes accessed | tf_op | source)
XLA Modules:
  0.0 121.6 jit_solution(12133176638432951235)
XLA Ops:
  0.6 118.2 %attention_backward.1 = (bf16[128,4096]{1,0:T(8,128)(2,1)}, bf16[128,512]{1,0:T(8,128)(2,1)}, bf16[128,2048]{1,0:T(8,128)(2,1)}, bf16[256,512]{1,0:T(8,128)(2,1)}) custom-call(s32[1,2048]{1,0:T(1,128)} %bitcast.2, s32[1,128]{1,0:T(1,128)} %bitcast.3, bf16[128,4096]{1,0:T(8,128)(2,1)} %q_ref.1, bf16[128,4096]{1,0:T(8,128)(2,1)} %g_ref.1, ...), custom_call_target="tpu_custom_call" | custom-call | flops 5368709120 | bytes 8388608 | tf_op jit(solution)/shard_map/attention_backward/pallas_call | solution.py:574
  118.8 2.8 %hand_over.1 = (bf16[128,4096]{1,0:T(8,128)(2,1)}, bf16[128,512]{1,0:T(8,128)(2,1)}, bf16[128,2048]{1,0:T(8,128)(2,1)}, bf16[256,512]{1,0:T(8,128)(2,1)}) custom-call(bf16[128,4096]{1,0:T(8,128)(2,1)} %get-tuple-element.8.refs_0_, bf16[128,512]{1,0:T(8,128)(2,1)} %get-tuple-element.9.refs_1_, bf16[128,2048]{1,0:T(8,128)(2,1)} %get-tuple-element.10.refs_2_, ...), custom_call_target="tpu_custom_call" | custom-call | tf_op jit(solution)/shard_map/hand_over/pallas_call | solution.py:641

commit v5 on v3

--- a/solution.py
+++ b/solution.py
@@ -447,11 +447,15 @@
     early = slab < slabs // 2
     gather_own(0)
     gather_forward(0)
+    if heads > 1:
+        gather_own(1)
     gather_cross(0)
     for d in range(1, mp_count):
         weight_copy(lax.rem(mine + d, mp_count), mine).start()
-    if heads > 1:
-        gather_own(1)
+
+    @pl.when(jnp.logical_not(early) & (heads > 2))
+    def _():
+        gather_own(min(2, heads - 1))
 
     def gather_early(c):
         gather_forward(c)
@@ -463,28 +467,34 @@
         gather_cross(c)
 
     repeat(1, jnp.where(early, heads, 1), gather_early)
+
+    late = jnp.logical_not(early)
 
     def head(c):
         prepare(c)
         gather_arrive(c)
 
-        @pl.when(c == min(1, heads - 1))
+        @pl.when(late & (c == 0) & (heads > 1))
+        def _():
+            gather_forward(min(1, heads - 1))
+
+        @pl.when(c > 0)
+        def _():
+            reduce_side(c - 1)
+
+        @pl.when(c == min(2, heads - 1))
         def _():
             x_start()
 
         first_pass(c)
 
-        @pl.when((c < heads - 1) & jnp.logical_not(early))
-        def _():
-            gather_forward(c + 1)
-
-            @pl.when(c < heads - 2)
+        @pl.when(late & (c < heads - 2))
+        def _():
+            gather_forward(c + 2)
+
+            @pl.when(c < heads - 3)
             def _():
-                gather_own(c + 2)
-
-        @pl.when(c > 0)
-        def _():
-            reduce_side(c - 1)
+                gather_own(c + 3)
 
         @pl.when(c > 1)
         def _():

time: 111 us -> 106 us (0.955)
  Pallas kernels: 110 us -> 105 us
    pallas_call x1, Pallas kernels: 107 us -> 102 us  [on_device(): pl.pallas_call(functools.partial(kernel, count, mp_count, heads, keep, x_...]
where the time goes in v5:
time: 106 us
  Pallas kernels  105 us (99%)
    pallas_call x1, Pallas kernels, on_device(): pl.pallas_call(functools.partial(kernel, count, mp_count, heads, keep, x_...  102 us
    pallas_call x1, Pallas kernels, on_device(): pl.pallas_call(hand_over, out_shape=tuple((jax.ShapeDtypeStruct(r.shape,...  2.8 us

profile of v5, /device:TPU:0, one launch (start us, length us, event | category | flops | bytes accessed | tf_op | source)
XLA Modules:
  0.0 105.8 jit_solution(16953662876575807711)
XLA Ops:
  0.6 102.4 %attention_backward.1 = (bf16[128,4096]{1,0:T(8,128)(2,1)}, bf16[128,512]{1,0:T(8,128)(2,1)}, bf16[128,2048]{1,0:T(8,128)(2,1)}, bf16[256,512]{1,0:T(8,128)(2,1)}) custom-call(s32[1,2048]{1,0:T(1,128)} %bitcast.2, s32[1,128]{1,0:T(1,128)} %bitcast.3, bf16[128,4096]{1,0:T(8,128)(2,1)} %q_ref.1, bf16[128,4096]{1,0:T(8,128)(2,1)} %g_ref.1, ...), custom_call_target="tpu_custom_call" | custom-call | flops 5368709120 | bytes 8388608 | tf_op jit(solution)/shard_map/attention_backward/pallas_call | solution.py:614
  103.0 2.8 %hand_over.1 = (bf16[128,4096]{1,0:T(8,128)(2,1)}, bf16[128,512]{1,0:T(8,128)(2,1)}, bf16[128,2048]{1,0:T(8,128)(2,1)}, bf16[256,512]{1,0:T(8,128)(2,1)}) custom-call(bf16[128,4096]{1,0:T(8,128)(2,1)} %get-tuple-element.8.refs_0_, bf16[128,512]{1,0:T(8,128)(2,1)} %get-tuple-element.9.refs_1_, bf16[128,2048]{1,0:T(8,128)(2,1)} %get-tuple-element.10.refs_2_, ...), custom_call_target="tpu_custom_call" | custom-call | tf_op jit(solution)/shard_map/hand_over/pallas_call | solution.py:681
